TPU v7x, 32 devices: a whole 2x2x4 slice. The times are simulated.
32 devices in a mesh: rowk: 4 (over z), colk: 8 (over y, x, core).
Axes of the slice: x: 2, y: 2, z: 4, core: 2. Of those that a mesh axis runs over, the one named last changes fastest.
Arguments:
- coarse_kernel: bfloat16 [64, 64, 128, 128], P(('rowk', 'colk')), may hold values from -0.03125 to 0.03125
- left_rotation: bfloat16 [128, 2, 128, 128], P('rowk'), may hold values from -0.5 to 0.5
- right_rotation: bfloat16 [128, 2, 128, 128], P('colk'), may hold values from -0.5 to 0.5
- fine_map: int32 [128], replicated, may hold values from 0 to 63, as said below
- coefficient_index: int32 [128, 128, 4], P('rowk', 'colk'), may hold values from 0 to 15, as said below
- coefficient_table: float32 [16], replicated, may hold values from 0.3 to 1
- trial_vectors: bfloat16 [64, 16384], P(None, 'colk'), may hold values from -6 to 6
Outputs:
- forward_image: bfloat16 [64, 16384], P(None, ('rowk', 'colk'))
- adjoint_image: bfloat16 [64, 16384], P('rowk', 'colk')
Inputs may be any that keep to these rules, and one draw needn't show every extreme that they name: `fine_map`: entry i is i // 2 or i // 2 - 1 and lies in the same aligned group of 8 coarse points as i // 2; it equals i // 2 where i // 2 is the first or the last of its group. `coefficient_index`: 0 marks an absent source; slot 0 is never 0.
All inputs are finite; a program needn't handle non-finite values.
Results may differ from a plain program's by a relative error of at most 0.018.
Values may be sent and summed in bfloat16 or wider, within the bound.
A program may use at most 128 MiB of HBM per device.

v0:
```python
import jax
import jax.numpy as jnp
from jax import lax
from jax.sharding import PartitionSpec as P


def shifted(value, axis, steps):
    count = lax.axis_size(axis)
    pairs = [(source, (source + steps) % count) for source in range(count)]
    return lax.ppermute(value, axis, pairs)


def finish_rows(gathered, weight_block, rotor_block):
    weight_turn = weight_block.transpose(0, 2, 1, 3)
    mixed = (
        weight_turn[:, :, :, 0, None, None] * gathered[:, :, :, 0]
        + weight_turn[:, :, :, 1, None, None] * gathered[:, :, :, 1]
    )
    mixed = mixed.astype(jnp.bfloat16)
    return jnp.einsum(
        "ipba,ipjbc->ijac", rotor_block, mixed, preferred_element_type=jnp.float32
    ).astype(jnp.bfloat16)


def body(
    coarse_kernel,
    left_rotation,
    right_rotation,
    fine_map,
    coefficient_index,
    coefficient_table,
    trial_vectors,
):
    n_rows = lax.axis_size("rowk")
    n_cols = lax.axis_size("colk")
    row_id = lax.axis_index("rowk")
    col_id = lax.axis_index("colk")
    coarse_total = coarse_kernel.shape[1]
    fine_rows = left_rotation.shape[0]
    fine_cols = right_rotation.shape[0]
    band_pairs = left_rotation.shape[2]
    vec_count = trial_vectors.shape[0]
    coarse_rows = coarse_total // n_rows
    coarse_cols = coarse_total // n_cols
    blocks = lax.all_to_all(coarse_kernel, "colk", split_axis=1, concat_axis=0, tiled=True)
    rim_row = shifted(blocks[0:1], "rowk", -1)
    taller = jnp.concatenate([blocks, rim_row], axis=0)
    rim_col = shifted(taller[:, 0:1], "colk", -1)
    local_blocks = jnp.concatenate([taller, rim_col], axis=1)
    offsets = jnp.arange(2, dtype=jnp.int32)
    row_base = (
        lax.dynamic_slice_in_dim(fine_map, row_id * fine_rows, fine_rows) - row_id * coarse_rows
    )
    col_base = (
        lax.dynamic_slice_in_dim(fine_map, col_id * fine_cols, fine_cols) - col_id * coarse_cols
    )
    row_source = row_base[:, None] + offsets[None, :]
    col_source = col_base[:, None] + offsets[None, :]
    entries = jnp.arange(coefficient_table.shape[0], dtype=jnp.int32)
    match = coefficient_index[..., None] == entries
    looked = jnp.sum(
        jnp.where(match, coefficient_table, jnp.zeros_like(coefficient_table)), axis=-1
    )
    weight = jnp.where(coefficient_index > 0, looked, jnp.zeros_like(looked))
    weight = weight.reshape(fine_rows, fine_cols, 2, 2)
    block_rows = 4
    block_count = fine_rows // block_rows
    row_blocks = row_source.reshape(block_count, block_rows, 2)
    weight_blocks = weight.reshape(block_count, block_rows, fine_cols, 2, 2)
    rotor_blocks = left_rotation.reshape(block_count, block_rows, 2, band_pairs, band_pairs)

    def build_rows(pieces):
        sources, weight_block, rotor_block = pieces
        picked = local_blocks[sources[:, :, None, None], col_source[None, None, :, :]]
        rotated = jnp.einsum(
            "ipjqab,jqbc->ipjqac", picked, right_rotation, preferred_element_type=jnp.float32
        ).astype(jnp.bfloat16)
        return finish_rows(rotated, weight_block, rotor_block)

    kernel = lax.map(build_rows, (row_blocks, weight_blocks, rotor_blocks))
    kernel = kernel.reshape(fine_rows, fine_cols, band_pairs, band_pairs)
    vec_cols = trial_vectors.reshape(vec_count, fine_cols, band_pairs)
    partial_value = jnp.einsum(
        "ijac,vjc->via", kernel, vec_cols, preferred_element_type=jnp.float32
    )
    partial_value = partial_value.reshape(vec_count, fine_rows * band_pairs)
    forward_image = lax.psum_scatter(
        partial_value.astype(jnp.bfloat16), "colk", scatter_dimension=1, tiled=True
    )
    row_image = lax.all_gather(forward_image, "colk", axis=1, tiled=True)
    row_three = row_image.reshape(vec_count, fine_rows, band_pairs)
    terms = jnp.einsum("ijac,via->vjc", kernel, row_three, preferred_element_type=jnp.float32)
    adjoint_image = lax.psum_scatter(
        terms.reshape(vec_count // n_rows * lax.axis_size("rowk"), fine_cols * band_pairs).astype(
            jnp.bfloat16
        ),
        "rowk",
        scatter_dimension=0,
        tiled=True,
    )
    return (forward_image, adjoint_image)


def solution(mesh):
    return jax.shard_map(
        body,
        mesh=mesh,
        in_specs=(
            P(("rowk", "colk"), None, None, None),
            P("rowk", None, None, None),
            P("colk", None, None, None),
            P(),
            P("rowk", "colk", None),
            P(),
            P(None, "colk"),
        ),
        out_specs=(P(None, ("rowk", "colk")), P("rowk", "colk")),
        check_vma=False,
    )
```

profile of v0, /device:TPU:0, one launch (start us, length us, event | category | flops | bytes accessed | tf_op | source)
XLA Modules:
  0.0 417.1 jit_solution(8320609945050592079)
XLA Ops:
  7.2 2.5 copy.55
  9.8 54.2 %all_to_all.18 = bf16[2,64,128,128]{3,2,0,1:T(8,128)(2,1)S(1)} all-to-all(bf16[2,64,128,128]{3,2,0,1:T(8,128)(2,1)S(1)} %copy.55), channel_id=1, replica_groups=mesh['rowk'=4,'colk'=8] {'colk'}, dimensions={1} | all-to-all | bytes 8388608 | tf_op jit(solution)/shard_map/all_to_all | solution.py:45
  64.0 0.6 copy.56
  64.6 1.9 copy-done.1
  66.5 3.7 collective-permute-start
  70.3 0.2 select_reduce_fusion
  70.6 4.5 %collective-permute-done = bf16[1,8,128,128]{3,2,1,0:T(8,128)(2,1)S(1)} collective-permute-done((bf16[1,8,128,128]{3,2,1,0:T(8,128)(2,1)S(1)}, bf16[1,8,128,128]{3,2,1,0:T(8,128)(2,1)S(1)}, u32[]{:S(2)}, u32[]{:S(2)}) %collective-permute-start) | collective-permute-done | bytes 262176 | tf_op jit(solution)/shard_map/ppermute | solution.py:10
  75.1 1.1 pad_maximum_fusion.1
  76.4 6.9 %collective-permute-done.1 = bf16[17,1,128,128]{3,2,1,0:T(8,128)(2,1)S(1)} collective-permute-done((bf16[17,1,128,128]{3,2,1,0:T(8,128)(2,1)S(1)}, bf16[17,1,128,128]{3,2,1,0:T(8,128)(2,1)S(1)}, u32[]{:S(2)}, u32[]{:S(2)}) %collective-permute-start.1) | collective-permute-done | bytes 557088 | tf_op jit(solution)/shard_map/ppermute | solution.py:10
  83.3 5.1 %pad_maximum_fusion = bf16[17,9,128,128]{3,2,1,0:T(8,128)(2,1)} fusion(bf16[17,1,128,128]{3,2,1,0:T(8,128)(2,1)S(1)} %collective-permute-done.1, bf16[1,8,128,128]{3,2,1,0:T(8,128)(2,1)S(1)} %collective-permute-done, bf16[16,8,128,128]{3,2,1,0:T(8,128)(2,1)} %bitcast.132), kind=kLoop, calls=%fused_computation.31 | loop fusion | flops 5013504 | bytes 10027008 | tf_op jit(solution)/shard_map/concatenate | solution.py:49
  88.4 234.8 %while.11 = (s32[]{:T(128)}, bf16[8,4,16,128,128]{3,4,2,1,0:T(8,128)(2,1)}, f32[8,4,16,2,2]{2,1,0,4,3:T(4,128)S(1)}, s32[8,4,2]{1,2,0:T(2,128)S(1)}, bf16[17,9,1...) while((s32[]{:T(128)}, ...), condition=%wide.region_2.3_spmd.clone, body=%wide.region_1.2_spmd.clone.sunk | while | flops 1628439040 | bytes 45366852 | solution.py:80
  88.7 0.1 reshape.94
  88.8 12.1 %gather_fusion = bf16[256,128,128]{2,1,0:T(8,128)(2,1)} fusion(bf16[17,9,128,128]{3,2,1,0:T(8,128)(2,1)} %get-tuple-element.181, s32[256]{0:T(256)S(1)} %reshape.94), kind=kCustom, calls=%fused_computation.clone.clone.1 | custom fusion | bytes 16779264 | tf_op jit(solution)/shard_map/while/body/eval_jaxpr/gather | solution.py:74
  100.9 9.0 %convert_bitcast_fusion.2 = bf16[4,2,16,2,128,128]{5,4,1,0,3,2:T(8,128)(2,1)} fusion(bf16[4,2,16,2,128,128]{5,4,3,2,1,0:T(8,128)(2,1)} %bitcast.127, bf16[16,2,128,128]{3,2,1,0:T(8,128)(2,1)S(1)} %get-tuple-element.182), kind=kOutput, calls=%fused_computation.8.clone.1 | convolution fusion | flops 1077936128 | bytes 17825792 | tf_op jit(solution)/shard_map/while/body/eval_jaxpr/ipjqab,jqbc->ipjqac/dot_general | solution.py:75
  110.1 7.6 %fusion.49 = bf16[8,4,16,128,128]{3,4,2,1,0:T(8,128)(2,1)} fusion(bf16[8,4,16,128,128]{3,4,2,1,0:T(8,128)(2,1)} %get-tuple-element.169, s32[]{:T(128)} %get-tuple-element.168, bf16[8,4,2,128,128]{4,3,2,1,0:T(8,128)(2,1)} %get-tuple-element.183, bf16[4,2,16,2,128,128]{5,4,1,0,3,2:T(8,128)(2,1)} %convert_bitcast_fusion.2, f32[4,2,16]{1,0,2:T(4,128)S(1)} %copy.104, ...), kind=kOutput, calls=%fused_computation.15.clone.1 | convolution fusion | flops 550502400 | bytes 10749952 | tf_op jit(solution)/shard_map/while/body/eval_jaxpr/ipba,ipjbc->ijac/dot_general | solution.py:20
  118.0 0.1 reshape.94
  118.1 12.1 %gather_fusion = bf16[256,128,128]{2,1,0:T(8,128)(2,1)} fusion(bf16[17,9,128,128]{3,2,1,0:T(8,128)(2,1)} %get-tuple-element.181, s32[256]{0:T(256)S(1)} %reshape.94), kind=kCustom, calls=%fused_computation.clone.clone.1 | custom fusion | bytes 16779264 | tf_op jit(solution)/shard_map/while/body/eval_jaxpr/gather | solution.py:74
  130.2 9.0 %convert_bitcast_fusion.2 = bf16[4,2,16,2,128,128]{5,4,1,0,3,2:T(8,128)(2,1)} fusion(bf16[4,2,16,2,128,128]{5,4,3,2,1,0:T(8,128)(2,1)} %bitcast.127, bf16[16,2,128,128]{3,2,1,0:T(8,128)(2,1)S(1)} %get-tuple-element.182), kind=kOutput, calls=%fused_computation.8.clone.1 | convolution fusion | flops 1077936128 | bytes 17825792 | tf_op jit(solution)/shard_map/while/body/eval_jaxpr/ipjqab,jqbc->ipjqac/dot_general | solution.py:75
  139.4 7.6 %fusion.49 = bf16[8,4,16,128,128]{3,4,2,1,0:T(8,128)(2,1)} fusion(bf16[8,4,16,128,128]{3,4,2,1,0:T(8,128)(2,1)} %get-tuple-element.169, s32[]{:T(128)} %get-tuple-element.168, bf16[8,4,2,128,128]{4,3,2,1,0:T(8,128)(2,1)} %get-tuple-element.183, bf16[4,2,16,2,128,128]{5,4,1,0,3,2:T(8,128)(2,1)} %convert_bitcast_fusion.2, f32[4,2,16]{1,0,2:T(4,128)S(1)} %copy.104, ...), kind=kOutput, calls=%fused_computation.15.clone.1 | convolution fusion | flops 550502400 | bytes 10749952 | tf_op jit(solution)/shard_map/while/body/eval_jaxpr/ipba,ipjbc->ijac/dot_general | solution.py:20
  147.3 0.1 reshape.94
  147.4 12.1 %gather_fusion = bf16[256,128,128]{2,1,0:T(8,128)(2,1)} fusion(bf16[17,9,128,128]{3,2,1,0:T(8,128)(2,1)} %get-tuple-element.181, s32[256]{0:T(256)S(1)} %reshape.94), kind=kCustom, calls=%fused_computation.clone.clone.1 | custom fusion | bytes 16779264 | tf_op jit(solution)/shard_map/while/body/eval_jaxpr/gather | solution.py:74
  159.5 9.0 %convert_bitcast_fusion.2 = bf16[4,2,16,2,128,128]{5,4,1,0,3,2:T(8,128)(2,1)} fusion(bf16[4,2,16,2,128,128]{5,4,3,2,1,0:T(8,128)(2,1)} %bitcast.127, bf16[16,2,128,128]{3,2,1,0:T(8,128)(2,1)S(1)} %get-tuple-element.182), kind=kOutput, calls=%fused_computation.8.clone.1 | convolution fusion | flops 1077936128 | bytes 17825792 | tf_op jit(solution)/shard_map/while/body/eval_jaxpr/ipjqab,jqbc->ipjqac/dot_general | solution.py:75
  168.7 7.6 %fusion.49 = bf16[8,4,16,128,128]{3,4,2,1,0:T(8,128)(2,1)} fusion(bf16[8,4,16,128,128]{3,4,2,1,0:T(8,128)(2,1)} %get-tuple-element.169, s32[]{:T(128)} %get-tuple-element.168, bf16[8,4,2,128,128]{4,3,2,1,0:T(8,128)(2,1)} %get-tuple-element.183, bf16[4,2,16,2,128,128]{5,4,1,0,3,2:T(8,128)(2,1)} %convert_bitcast_fusion.2, f32[4,2,16]{1,0,2:T(4,128)S(1)} %copy.104, ...), kind=kOutput, calls=%fused_computation.15.clone.1 | convolution fusion | flops 550502400 | bytes 10749952 | tf_op jit(solution)/shard_map/while/body/eval_jaxpr/ipba,ipjbc->ijac/dot_general | solution.py:20
  176.6 0.1 reshape.94
  176.7 12.5 %gather_fusion = bf16[256,128,128]{2,1,0:T(8,128)(2,1)} fusion(bf16[17,9,128,128]{3,2,1,0:T(8,128)(2,1)} %get-tuple-element.181, s32[256]{0:T(256)S(1)} %reshape.94), kind=kCustom, calls=%fused_computation.clone.clone.1 | custom fusion | bytes 16779264 | tf_op jit(solution)/shard_map/while/body/eval_jaxpr/gather | solution.py:74
  189.2 9.0 %convert_bitcast_fusion.2 = bf16[4,2,16,2,128,128]{5,4,1,0,3,2:T(8,128)(2,1)} fusion(bf16[4,2,16,2,128,128]{5,4,3,2,1,0:T(8,128)(2,1)} %bitcast.127, bf16[16,2,128,128]{3,2,1,0:T(8,128)(2,1)S(1)} %get-tuple-element.182), kind=kOutput, calls=%fused_computation.8.clone.1 | convolution fusion | flops 1077936128 | bytes 17825792 | tf_op jit(solution)/shard_map/while/body/eval_jaxpr/ipjqab,jqbc->ipjqac/dot_general | solution.py:75
  198.4 7.6 %fusion.49 = bf16[8,4,16,128,128]{3,4,2,1,0:T(8,128)(2,1)} fusion(bf16[8,4,16,128,128]{3,4,2,1,0:T(8,128)(2,1)} %get-tuple-element.169, s32[]{:T(128)} %get-tuple-element.168, bf16[8,4,2,128,128]{4,3,2,1,0:T(8,128)(2,1)} %get-tuple-element.183, bf16[4,2,16,2,128,128]{5,4,1,0,3,2:T(8,128)(2,1)} %convert_bitcast_fusion.2, f32[4,2,16]{1,0,2:T(4,128)S(1)} %copy.104, ...), kind=kOutput, calls=%fused_computation.15.clone.1 | convolution fusion | flops 550502400 | bytes 10749952 | tf_op jit(solution)/shard_map/while/body/eval_jaxpr/ipba,ipjbc->ijac/dot_general | solution.py:20
  206.3 0.1 reshape.94
  206.4 11.7 %gather_fusion = bf16[256,128,128]{2,1,0:T(8,128)(2,1)} fusion(bf16[17,9,128,128]{3,2,1,0:T(8,128)(2,1)} %get-tuple-element.181, s32[256]{0:T(256)S(1)} %reshape.94), kind=kCustom, calls=%fused_computation.clone.clone.1 | custom fusion | bytes 16779264 | tf_op jit(solution)/shard_map/while/body/eval_jaxpr/gather | solution.py:74
  218.1 9.0 %convert_bitcast_fusion.2 = bf16[4,2,16,2,128,128]{5,4,1,0,3,2:T(8,128)(2,1)} fusion(bf16[4,2,16,2,128,128]{5,4,3,2,1,0:T(8,128)(2,1)} %bitcast.127, bf16[16,2,128,128]{3,2,1,0:T(8,128)(2,1)S(1)} %get-tuple-element.182), kind=kOutput, calls=%fused_computation.8.clone.1 | convolution fusion | flops 1077936128 | bytes 17825792 | tf_op jit(solution)/shard_map/while/body/eval_jaxpr/ipjqab,jqbc->ipjqac/dot_general | solution.py:75
  227.3 7.6 %fusion.49 = bf16[8,4,16,128,128]{3,4,2,1,0:T(8,128)(2,1)} fusion(bf16[8,4,16,128,128]{3,4,2,1,0:T(8,128)(2,1)} %get-tuple-element.169, s32[]{:T(128)} %get-tuple-element.168, bf16[8,4,2,128,128]{4,3,2,1,0:T(8,128)(2,1)} %get-tuple-element.183, bf16[4,2,16,2,128,128]{5,4,1,0,3,2:T(8,128)(2,1)} %convert_bitcast_fusion.2, f32[4,2,16]{1,0,2:T(4,128)S(1)} %copy.104, ...), kind=kOutput, calls=%fused_computation.15.clone.1 | convolution fusion | flops 550502400 | bytes 10749952 | tf_op jit(solution)/shard_map/while/body/eval_jaxpr/ipba,ipjbc->ijac/dot_general | solution.py:20
  235.2 0.1 reshape.94
  235.4 12.1 %gather_fusion = bf16[256,128,128]{2,1,0:T(8,128)(2,1)} fusion(bf16[17,9,128,128]{3,2,1,0:T(8,128)(2,1)} %get-tuple-element.181, s32[256]{0:T(256)S(1)} %reshape.94), kind=kCustom, calls=%fused_computation.clone.clone.1 | custom fusion | bytes 16779264 | tf_op jit(solution)/shard_map/while/body/eval_jaxpr/gather | solution.py:74
  247.5 9.0 %convert_bitcast_fusion.2 = bf16[4,2,16,2,128,128]{5,4,1,0,3,2:T(8,128)(2,1)} fusion(bf16[4,2,16,2,128,128]{5,4,3,2,1,0:T(8,128)(2,1)} %bitcast.127, bf16[16,2,128,128]{3,2,1,0:T(8,128)(2,1)S(1)} %get-tuple-element.182), kind=kOutput, calls=%fused_computation.8.clone.1 | convolution fusion | flops 1077936128 | bytes 17825792 | tf_op jit(solution)/shard_map/while/body/eval_jaxpr/ipjqab,jqbc->ipjqac/dot_general | solution.py:75
  256.7 7.6 %fusion.49 = bf16[8,4,16,128,128]{3,4,2,1,0:T(8,128)(2,1)} fusion(bf16[8,4,16,128,128]{3,4,2,1,0:T(8,128)(2,1)} %get-tuple-element.169, s32[]{:T(128)} %get-tuple-element.168, bf16[8,4,2,128,128]{4,3,2,1,0:T(8,128)(2,1)} %get-tuple-element.183, bf16[4,2,16,2,128,128]{5,4,1,0,3,2:T(8,128)(2,1)} %convert_bitcast_fusion.2, f32[4,2,16]{1,0,2:T(4,128)S(1)} %copy.104, ...), kind=kOutput, calls=%fused_computation.15.clone.1 | convolution fusion | flops 550502400 | bytes 10749952 | tf_op jit(solution)/shard_map/while/body/eval_jaxpr/ipba,ipjbc->ijac/dot_general | solution.py:20
  264.5 0.1 reshape.94
  264.7 12.1 %gather_fusion = bf16[256,128,128]{2,1,0:T(8,128)(2,1)} fusion(bf16[17,9,128,128]{3,2,1,0:T(8,128)(2,1)} %get-tuple-element.181, s32[256]{0:T(256)S(1)} %reshape.94), kind=kCustom, calls=%fused_computation.clone.clone.1 | custom fusion | bytes 16779264 | tf_op jit(solution)/shard_map/while/body/eval_jaxpr/gather | solution.py:74
  276.8 9.0 %convert_bitcast_fusion.2 = bf16[4,2,16,2,128,128]{5,4,1,0,3,2:T(8,128)(2,1)} fusion(bf16[4,2,16,2,128,128]{5,4,3,2,1,0:T(8,128)(2,1)} %bitcast.127, bf16[16,2,128,128]{3,2,1,0:T(8,128)(2,1)S(1)} %get-tuple-element.182), kind=kOutput, calls=%fused_computation.8.clone.1 | convolution fusion | flops 1077936128 | bytes 17825792 | tf_op jit(solution)/shard_map/while/body/eval_jaxpr/ipjqab,jqbc->ipjqac/dot_general | solution.py:75
  286.0 7.6 %fusion.49 = bf16[8,4,16,128,128]{3,4,2,1,0:T(8,128)(2,1)} fusion(bf16[8,4,16,128,128]{3,4,2,1,0:T(8,128)(2,1)} %get-tuple-element.169, s32[]{:T(128)} %get-tuple-element.168, bf16[8,4,2,128,128]{4,3,2,1,0:T(8,128)(2,1)} %get-tuple-element.183, bf16[4,2,16,2,128,128]{5,4,1,0,3,2:T(8,128)(2,1)} %convert_bitcast_fusion.2, f32[4,2,16]{1,0,2:T(4,128)S(1)} %copy.104, ...), kind=kOutput, calls=%fused_computation.15.clone.1 | convolution fusion | flops 550502400 | bytes 10749952 | tf_op jit(solution)/shard_map/while/body/eval_jaxpr/ipba,ipjbc->ijac/dot_general | solution.py:20
  294.0 12.5 %gather_fusion = bf16[256,128,128]{2,1,0:T(8,128)(2,1)} fusion(bf16[17,9,128,128]{3,2,1,0:T(8,128)(2,1)} %get-tuple-element.181, s32[256]{0:T(256)S(1)} %reshape.94), kind=kCustom, calls=%fused_computation.clone.clone.1 | custom fusion | bytes 16779264 | tf_op jit(solution)/shard_map/while/body/eval_jaxpr/gather | solution.py:74
  306.4 9.0 %convert_bitcast_fusion.2 = bf16[4,2,16,2,128,128]{5,4,1,0,3,2:T(8,128)(2,1)} fusion(bf16[4,2,16,2,128,128]{5,4,3,2,1,0:T(8,128)(2,1)} %bitcast.127, bf16[16,2,128,128]{3,2,1,0:T(8,128)(2,1)S(1)} %get-tuple-element.182), kind=kOutput, calls=%fused_computation.8.clone.1 | convolution fusion | flops 1077936128 | bytes 17825792 | tf_op jit(solution)/shard_map/while/body/eval_jaxpr/ipjqab,jqbc->ipjqac/dot_general | solution.py:75
  315.6 7.6 %fusion.49 = bf16[8,4,16,128,128]{3,4,2,1,0:T(8,128)(2,1)} fusion(bf16[8,4,16,128,128]{3,4,2,1,0:T(8,128)(2,1)} %get-tuple-element.169, s32[]{:T(128)} %get-tuple-element.168, bf16[8,4,2,128,128]{4,3,2,1,0:T(8,128)(2,1)} %get-tuple-element.183, bf16[4,2,16,2,128,128]{5,4,1,0,3,2:T(8,128)(2,1)} %convert_bitcast_fusion.2, f32[4,2,16]{1,0,2:T(4,128)S(1)} %copy.104, ...), kind=kOutput, calls=%fused_computation.15.clone.1 | convolution fusion | flops 550502400 | bytes 10749952 | tf_op jit(solution)/shard_map/while/body/eval_jaxpr/ipba,ipjbc->ijac/dot_general | solution.py:20
  323.2 7.4 %fusion.24 = bf16[32,8,8,128]{3,2,1,0:T(8,128)(2,1)S(1)} fusion(bf16[32,16,128,128]{2,3,1,0:T(8,128)(2,1)} %bitcast.128, bf16[64,2048]{1,0:T(8,128)(2,1)S(1)} %copy-done), kind=kOutput, calls=%fused_computation.36 | convolution fusion | flops 1074003968 | bytes 17563648 | tf_op jit(solution)/shard_map/ijac,vjc->via/dot_general | solution.py:83
  330.7 0.9 copy.93
  331.6 37.3 %reduce-scatter.3.cloned.1.call-done = bf16[64,512]{1,0:T(8,128)(2,1)} async-done(((bf16[64,4096]{1,0:T(8,128)(2,1)}), bf16[64,512]{1,0:T(8,128)(2,1)}) %reduce-scatter.3.cloned.1.call-update) | async-done | bytes 65552 | tf_op jit(solution)/shard_map/reduce_scatter | solution.py:87
  369.0 10.0 %all_gather.3 = bf16[64,4096]{1,0:T(8,128)(2,1)S(1)} all-gather(bf16[64,512]{1,0:T(8,128)(2,1)} %reduce-scatter.3.cloned.1.call-done), channel_id=1, replica_groups=mesh['rowk'=4,'colk'=8] {'colk'}, dimensions={1}, use_global_device_ids=true | all-gather | bytes 589824 | tf_op jit(solution)/shard_map/all_gather | solution.py:90
  378.9 11.6 %fusion.22 = bf16[64,2048]{1,0:T(8,128)(2,1)} fusion(bf16[2048,128,32]{1,0,2:T(8,128)(2,1)} %bitcast.129, bf16[64,4096]{1,0:T(8,128)(2,1)S(1)} %all_gather.3), kind=kOutput, calls=%fused_computation.33 | convolution fusion | flops 1073872896 | bytes 17563648 | tf_op jit(solution)/shard_map/ijac,via->vjc/dot_general | solution.py:92
  390.5 19.8 %reduce-scatter.5.cloned.1.call-done = bf16[16,2048]{1,0:T(8,128)(2,1)} async-done(((bf16[64,2048]{1,0:T(8,128)(2,1)}), bf16[16,2048]{1,0:T(8,128)(2,1)}) %reduce-scatter.5.cloned.1.call-update) | async-done | bytes 65552 | tf_op jit(solution)/shard_map/reduce_scatter | solution.py:93
  (97 shorter events, 4.6 us)
Async XLA Ops:
  7.2 316.1 %copy-start = (bf16[64,2048]{1,0:T(8,128)(2,1)S(1)}, bf16[64,2048]{1,0:T(8,128)(2,1)}, u32[]{:S(2)}) copy-start(bf16[64,2048]{1,0:T(8,128)(2,1)} %param.15) | copy-start | bytes 786436
  7.2 361.8 %reduce-scatter.3.cloned.1.call-start = ((), (), s32[]{:S(2)}) async-start(), calls=%async_computation.3 | async-start | bytes 589824 | tf_op jit(solution)/shard_map/reduce_scatter | solution.py:87
  9.8 60.4 %copy-start.4 = (s32[128]{0:T(128)S(1)}, s32[128]{0:T(128)}, u32[]{:S(2)}) copy-start(s32[128]{0:T(128)} %param.12) | copy-start | bytes 1540
  9.8 60.6 %copy-start.3 = (s32[32,16,4]{0,2,1:T(4,128)S(1)}, s32[32,16,4]{0,2,1:T(4,128)}, u32[]{:S(2)}) copy-start(s32[32,16,4]{0,2,1:T(4,128)} %param.13) | copy-start | bytes 24580
  9.8 60.5 %copy-start.5 = (f32[16]{0:T(128)S(1)}, f32[16]{0:T(128)}, u32[]{:S(2)}) copy-start(f32[16]{0:T(128)} %param.14) | copy-start | bytes 196
  64.5 1.9 copy-start.1
  64.6 23.9 %copy-start.2 = (bf16[16,2,128,128]{3,2,1,0:T(8,128)(2,1)S(1)}, bf16[16,2,128,128]{3,2,1,0:T(8,128)(2,1)}, u32[]{:S(2)}) copy-start(bf16[16,2,128,128]{3,2,1,0:T(8,128)(2,1)} %param.11) | copy-start | bytes 3145732
  66.5 8.6 %collective-permute-start = (bf16[1,8,128,128]{3,2,1,0:T(8,128)(2,1)S(1)}, bf16[1,8,128,128]{3,2,1,0:T(8,128)(2,1)S(1)}, u32[]{:S(2)}, u32[]{:S(2)}) collective-permute-start(bf16[1,8,128,128]{3,2,1,0:T(8,128)(2,1)S(1)} %slice.30), channel_id=1, source_target_pairs={{0,24},{8,0},{16,8},{24,16},{1,25},{9,1},{17,9},{25,17},{2,26},{10... | collective-permute-start | bytes 786440 | tf_op jit(solution)/shard_map/ppermute | solution.py:10
  76.2 7.1 %collective-permute-start.1 = (bf16[17,1,128,128]{3,2,1,0:T(8,128)(2,1)S(1)}, bf16[17,1,128,128]{3,2,1,0:T(8,128)(2,1)S(1)}, u32[]{:S(2)}, u32[]{:S(2)}) collective-permute-start(bf16[17,1,128,128]{3,2,1,0:T(8,128)(2,1)S(1)} %pad_maximum_fusion.1), channel_id=1, source_target_pairs={{0,7},{1,0},{2,1},{3,2},{4,3},{5,4},{6,5},{7,6},{8,15},{9,8},{10,9... | collective-permute-start | bytes 1671176 | tf_op jit(solution)/shard_map/ppermute | solution.py:10
  331.6 78.7 %reduce-scatter.5.cloned.1.call-start = ((), (), s32[]{:S(2)}) async-start(), calls=%async_computation.4 | async-start | bytes 327680 | tf_op jit(solution)/shard_map/reduce_scatter | solution.py:93
Sparse Core Ops, SparseCore 0:
  331.7 37.1 reduce-scatter.2
  390.7 19.5 reduce-scatter.4
where the time goes:
time: 419 us; the launch traced here: 417 us
  matrix products  152 us (36%)
  local copies, waits for them, and re-layouts  107 us (26%)
  waiting for transfers between devices  68.5 us (16%)
  blocking collectives  64.1 us (15%)
  between operations  14.1 us (3%)
  other arithmetic  7.89 us (2%)
    gather x8, local copies, waits for them, and re-layouts, build_rows(): local_blocks[sources[:, :, None, None], col_source[None, None, :, :]]  97 us
    dot_general x8, matrix products, build_rows(): jnp.einsum('ipjqab,jqbc->ipjqac', picked, right_rotation, preferred_eleme...  71.8 us
    dot_general x8, matrix products, finish_rows(): jnp.einsum('ipba,ipjbc->ijac', rotor_block, mixed, preferred_element_type...  61 us
    all_to_all x1, blocking collectives, body(): lax.all_to_all(coarse_kernel, 'colk', split_axis=1, concat_axis=0, tiled=...  54.2 us
    reduce_scatter x1, waiting for transfers between devices, body(): lax.psum_scatter(partial_value.astype(jnp.bfloat16), 'colk', scatter_dime...  37.3 us
    reduce_scatter x1, waiting for transfers between devices, body(): lax.psum_scatter(terms.reshape(vec_count // n_rows * lax.axis_size('rowk'...  19.8 us
    dot_general x1, matrix products, body(): jnp.einsum('ijac,via->vjc', kernel, row_three, preferred_element_type=jnp...  11.6 us
    ppermute x2, waiting for transfers between devices, shifted(): return lax.ppermute(value, axis, pairs)  11.4 us
  transfers between devices with their start and end apart: 4, of which 4 were waited for; matrix products, arithmetic and copies ran while one was open for 0% of the time, Pallas kernels for 0%

commit v1 on v0

v1 whole, which is shorter than its diff:
```python
import functools

import jax
import jax.numpy as jnp
from jax import lax
from jax.experimental import pallas as pl
from jax.experimental.pallas import tpu as pltpu
from jax.sharding import PartitionSpec as P

MESH = pl.DeviceIdType.MESH
F32 = jnp.float32
BF16 = jnp.bfloat16


def dot_nt(left, right):
    return lax.dot_general(left, right, (((1,), (1,)), ((), ())), preferred_element_type=F32)


def dot_nn(left, right):
    return lax.dot_general(left, right, (((1,), (0,)), ((), ())), preferred_element_type=F32)


def operator_kernel(
    sizes,
    kernel_ref, left_ref, right_ref, row_pick, col_pick, mix_ref, vec_ref,
    forward_ref, adjoint_ref,
    blocks, turned, wide, coarse_image, part_out, part_in, gathered, lifted, wide_back, slot_image,
    back_out, back_in,
    own_sem, main_send, main_recv, rim_send, rim_recv, relay_send, relay_recv,
    part_send, part_recv, row_send, row_recv, back_send, back_recv,
):
    n_rows, n_cols, held, p_count, q_count, fine_rows, fine_cols, nb, vecs, j_pad = sizes
    row_id, col_id = lax.axis_index("rowk"), lax.axis_index("colk")
    coarse_cols = q_count - 1
    chunk = fine_rows // n_cols
    share = vecs // n_rows

    def column_peer(offset):
        return lax.rem(col_id + offset, n_cols)

    def row_peer(offset):
        return lax.rem(row_id + offset, n_rows)

    barrier = pltpu.get_barrier_semaphore()
    for offset in range(1, n_cols):
        pl.semaphore_signal(barrier, inc=1, device_id=(row_id, column_peer(offset)), device_id_type=MESH)
    for offset in range(1, n_rows):
        pl.semaphore_signal(barrier, inc=1, device_id=(row_peer(offset), col_id), device_id_type=MESH)
    pl.semaphore_wait(barrier, n_cols - 1 + n_rows - 1)

    sends = []
    for row in range(held):
        place = col_id * held + row
        for offset in range(1, n_cols):
            peer = column_peer(offset)
            rim = lax.rem(peer + 1, n_cols) * coarse_cols
            at = row * n_cols + offset
            sends.append(pltpu.make_async_remote_copy(
                src_ref=kernel_ref.at[row, pl.ds(peer * coarse_cols, coarse_cols)],
                dst_ref=blocks.at[pl.ds(0, coarse_cols), place],
                send_sem=main_send.at[at], recv_sem=main_recv.at[place],
                device_id=(row_id, peer), device_id_type=MESH,
            ))
            sends.append(pltpu.make_async_remote_copy(
                src_ref=kernel_ref.at[row, rim], dst_ref=blocks.at[coarse_cols, place],
                send_sem=rim_send.at[at], recv_sem=rim_recv.at[place],
                device_id=(row_id, peer), device_id_type=MESH,
            ))
    own = []
    for row in range(held):
        place = col_id * held + row
        rim = lax.rem(col_id + 1, n_cols) * coarse_cols
        own.append(pltpu.make_async_copy(
            kernel_ref.at[row, pl.ds(col_id * coarse_cols, coarse_cols)],
            blocks.at[pl.ds(0, coarse_cols), place], own_sem.at[row, 0],
        ))
        own.append(pltpu.make_async_copy(
            kernel_ref.at[row, rim], blocks.at[coarse_cols, place], own_sem.at[row, 1],
        ))
    for copy in sends + own:
        copy.start()

    turned[...] = jnp.zeros_like(turned)
    lifted[...] = jnp.zeros_like(lifted)

    def turn(j, carry):
        vec = vec_ref[:, pl.ds(pl.multiple_of(j * nb, nb), nb)]
        for slot in range(3):
            side = jnp.clip(col_pick[j] - 1 + slot, 0, 1)
            turned[j + 2, slot] = dot_nt(vec, right_ref[j, side])
        return carry

    lax.fori_loop(0, fine_cols, turn, 0)

    def scale(i, slot, j, other):
        return mix_ref[((i * 3 + slot) * j_pad + j) * 3 + other]

    half = vecs // 2

    def widen(step, carry):
        q, p = step // p_count, step % p_count
        for part in range(2):
            rows = pl.ds(part * half, half)
            tiles = [turned[2 * q + b, 2 - b // 2, rows] for b in range(6)]
            for a in range(6):
                total = scale(2 * p + a, 2 - a // 2, 2 * q, 2) * tiles[0]
                for b in range(1, 6):
                    total += scale(2 * p + a, 2 - a // 2, 2 * q + b, 2 - b // 2) * tiles[b]
                wide[p, pl.ds(a * vecs + part * half, half), pl.ds(pl.multiple_of(q * nb, nb), nb)] = total.astype(BF16)
        return carry

    lax.fori_loop(0, p_count * q_count, widen, 0)

    def contract(p):
        matrix = jnp.concatenate([blocks[q, p] for q in range(q_count)], axis=1)
        coarse_image[p] = dot_nt(wide[p], matrix).astype(BF16)

    relay = pltpu.make_async_remote_copy(
        src_ref=blocks.at[:, 0], dst_ref=blocks.at[:, p_count - 1],
        send_sem=relay_send, recv_sem=relay_recv,
        device_id=(row_peer(n_rows - 1), col_id), device_id_type=MESH,
    )

    def pass_on(place):
        @pl.when(place == 0)
        def _():
            relay.start()

    def take(step, carry):
        row, offset = step // (n_cols - 1), step % (n_cols - 1) + 1
        source = lax.rem(col_id - offset + n_cols, n_cols)
        place = source * held + row
        pltpu.make_async_remote_copy(
            src_ref=blocks.at[pl.ds(0, coarse_cols), place], dst_ref=blocks.at[pl.ds(0, coarse_cols), place],
            send_sem=main_send.at[0], recv_sem=main_recv.at[place],
            device_id=(row_id, source), device_id_type=MESH,
        ).wait_recv()
        pltpu.make_async_remote_copy(
            src_ref=blocks.at[coarse_cols, place], dst_ref=blocks.at[coarse_cols, place],
            send_sem=rim_send.at[0], recv_sem=rim_recv.at[place],
            device_id=(row_id, source), device_id_type=MESH,
        ).wait_recv()
        pass_on(place)
        contract(place)
        return carry

    for copy in own:
        copy.wait()
    pass_on(col_id * held)
    for row in range(held):
        contract(col_id * held + row)
    lax.fori_loop(0, held * (n_cols - 1), take, 0)
    relay.wait_recv()
    contract(p_count - 1)

    def part_of(target):
        for k in range(chunk):
            i = target * chunk + k
            total = None
            for slot in range(3):
                side = jnp.clip(row_pick[i] - 1 + slot, 0, 1)
                place = jnp.maximum(i // 2 - 1 + slot, 0)
                at = (2 - slot) * 2 + i % 2
                image = coarse_image[place, pl.ds(pl.multiple_of(at * vecs, vecs), vecs)]
                term = dot_nn(image, left_ref[i, side])
                usable = jnp.where(i // 2 - 1 + slot >= 0, 1.0, 0.0)
                total = term * usable if total is None else total + term
            part_out[target, :, pl.ds(k * nb, nb)] = total.astype(BF16)

    def part_copy(offset):
        peer = column_peer(offset)
        return pltpu.make_async_remote_copy(
            src_ref=part_out.at[peer], dst_ref=part_in.at[col_id],
            send_sem=part_send.at[offset], recv_sem=part_recv.at[col_id],
            device_id=(row_id, peer), device_id_type=MESH,
        )

    def send_part(offset, carry):
        part_of(column_peer(offset))
        part_copy(offset).start()
        return carry

    lax.fori_loop(1, n_cols, send_part, 0)
    part_of(col_id)

    def add_part(offset, total):
        source = column_peer(offset)
        pltpu.make_async_remote_copy(
            src_ref=part_in.at[source], dst_ref=part_in.at[source],
            send_sem=part_send.at[0], recv_sem=part_recv.at[source],
            device_id=(row_id, source), device_id_type=MESH,
        ).wait_recv()
        return total + part_in[source].astype(F32)

    total = part_out[col_id].astype(F32)
    for offset in range(1, n_cols):
        total = add_part(offset, total)
    image = total.astype(BF16)
    forward_ref[...] = image
    gathered[col_id] = image

    def row_copy(offset):
        return pltpu.make_async_remote_copy(
            src_ref=gathered.at[col_id], dst_ref=gathered.at[col_id],
            send_sem=row_send.at[offset], recv_sem=row_recv.at[col_id],
            device_id=(row_id, column_peer(offset)), device_id_type=MESH,
        )

    for offset in range(1, n_cols):
        row_copy(offset).start()

    def lift(source):
        for k in range(chunk):
            i = source * chunk + k
            piece = gathered[source, :, pl.ds(k * nb, nb)]
            for slot in range(3):
                side = jnp.clip(row_pick[i] - 1 + slot, 0, 1)
                lifted[i + 2, slot] = dot_nt(piece, left_ref[i, side])

    lift(col_id)

    def lift_next(offset, carry):
        source = lax.rem(col_id - offset + n_cols, n_cols)
        pltpu.make_async_remote_copy(
            src_ref=gathered.at[source], dst_ref=gathered.at[source],
            send_sem=row_send.at[0], recv_sem=row_recv.at[source],
            device_id=(row_id, source), device_id_type=MESH,
        ).wait_recv()
        lift(source)
        return carry

    lax.fori_loop(1, n_cols, lift_next, 0)

    def back(q, carry):
        def mix(p, inner):
            for part in range(2):
                rows = pl.ds(part * half, half)
                tiles = [lifted[2 * p + a, 2 - a // 2, rows] for a in range(6)]
                for b in range(6):
                    total = scale(2 * p, 2, 2 * q + b, 2 - b // 2) * tiles[0]
                    for a in range(1, 6):
                        total += scale(2 * p + a, 2 - a // 2, 2 * q + b, 2 - b // 2) * tiles[a]
                    wide_back[pl.ds(b * vecs + part * half, half), pl.ds(pl.multiple_of(p * nb, nb), nb)] = total.astype(BF16)
            return inner

        lax.fori_loop(0, p_count, mix, 0)
        matrix = jnp.concatenate([blocks[q, p] for p in range(p_count)], axis=0)
        slot_image[q] = dot_nn(wide_back[...], matrix).astype(BF16)
        return carry

    lax.fori_loop(0, q_count, back, 0)

    def finish(j, carry):
        total = None
        for slot in range(3):
            side = jnp.clip(col_pick[j] - 1 + slot, 0, 1)
            place = jnp.maximum(j // 2 - 1 + slot, 0)
            at = (2 - slot) * 2 + j % 2
            image = slot_image[place, pl.ds(pl.multiple_of(at * vecs, vecs), vecs)]
            term = dot_nn(image, right_ref[j, side])
            usable = jnp.where(j // 2 - 1 + slot >= 0, 1.0, 0.0)
            total = term * usable if total is None else total + term
        for target in range(n_rows):
            back_out[target, :, pl.ds(pl.multiple_of(j * nb, nb), nb)] = (
                total[target * share:(target + 1) * share].astype(BF16)
            )
        return carry

    lax.fori_loop(0, fine_cols, finish, 0)

    def back_copy(offset):
        peer = row_peer(offset)
        return pltpu.make_async_remote_copy(
            src_ref=back_out.at[peer], dst_ref=back_in.at[row_id],
            send_sem=back_send.at[offset], recv_sem=back_recv.at[row_id],
            device_id=(peer, col_id), device_id_type=MESH,
        )

    for offset in range(1, n_rows):
        back_copy(offset).start()
    total = back_out[row_id].astype(F32)
    for offset in range(1, n_rows):
        source = row_peer(offset)
        pltpu.make_async_remote_copy(
            src_ref=back_in.at[source], dst_ref=back_in.at[source],
            send_sem=back_send.at[0], recv_sem=back_recv.at[source],
            device_id=(source, col_id), device_id_type=MESH,
        ).wait_recv()
        total = total + back_in[source].astype(F32)
    adjoint_ref[...] = total.astype(BF16)

    for copy in sends:
        copy.wait_send()
    relay.wait_send()
    for offset in range(1, n_cols):
        part_copy(offset).wait_send()
        row_copy(offset).wait_send()
    for offset in range(1, n_rows):
        back_copy(offset).wait_send()


def body(
    coarse_kernel,
    left_rotation,
    right_rotation,
    fine_map,
    coefficient_index,
    coefficient_table,
    trial_vectors,
):
    n_rows = lax.axis_size("rowk")
    n_cols = lax.axis_size("colk")
    row_id = lax.axis_index("rowk")
    col_id = lax.axis_index("colk")
    held, coarse_total = coarse_kernel.shape[:2]
    fine_rows = left_rotation.shape[0]
    fine_cols = right_rotation.shape[0]
    nb = left_rotation.shape[2]
    vecs = trial_vectors.shape[0]
    p_count = coarse_total // n_rows + 1
    q_count = coarse_total // n_cols + 1
    chunk = fine_rows // n_cols
    share = vecs // n_rows

    pick = jnp.arange(fine_map.shape[0], dtype=jnp.int32) // 2 - fine_map
    row_pick = lax.dynamic_slice_in_dim(pick, row_id * fine_rows, fine_rows)
    col_pick = lax.dynamic_slice_in_dim(pick, col_id * fine_cols, fine_cols)

    entries = jnp.arange(coefficient_table.shape[0], dtype=jnp.int32)
    match = (coefficient_index[..., None] == entries) & (coefficient_index[..., None] > 0)
    weight = jnp.sum(jnp.where(match, coefficient_table, 0.0), axis=-1)
    slots = jnp.arange(3, dtype=jnp.int32)
    row_side = row_pick[:, None] - 1 + slots
    col_side = col_pick[:, None] - 1 + slots
    mix = jnp.zeros((fine_rows, 3, fine_cols, 3), F32)
    for dp in range(2):
        for dq in range(2):
            here = (row_side == dp)[:, :, None, None] & (col_side == dq)[None, None, :, :]
            mix = mix + jnp.where(here, weight[:, None, :, None, 2 * dp + dq], 0.0)
    mix = jnp.pad(mix, ((2, 4), (0, 0), (2, 4), (0, 0)))
    i_pad, j_pad = fine_rows + 6, fine_cols + 6

    sizes = (n_rows, n_cols, held, p_count, q_count, fine_rows, fine_cols, nb, vecs, j_pad)
    vmem = pl.BlockSpec(memory_space=pltpu.VMEM)
    smem = pl.BlockSpec(memory_space=pltpu.SMEM)
    dma = pltpu.SemaphoreType.DMA
    return pl.pallas_call(
        functools.partial(operator_kernel, sizes),
        out_shape=(
            jax.ShapeDtypeStruct((vecs, chunk * nb), BF16),
            jax.ShapeDtypeStruct((share, fine_cols * nb), BF16),
        ),
        in_specs=[pl.BlockSpec(memory_space=pl.ANY), vmem, vmem, smem, smem, smem, vmem],
        out_specs=(vmem, vmem),
        scratch_shapes=[
            pltpu.VMEM((q_count, p_count, nb, nb), BF16),
            pltpu.VMEM((j_pad, 3, vecs, nb), F32),
            pltpu.VMEM((p_count, 6 * vecs, q_count * nb), BF16),
            pltpu.VMEM((p_count, 6 * vecs, nb), BF16),
            pltpu.VMEM((n_cols, vecs, chunk * nb), BF16),
            pltpu.VMEM((n_cols, vecs, chunk * nb), BF16),
            pltpu.VMEM((n_cols, vecs, chunk * nb), BF16),
            pltpu.VMEM((i_pad, 3, vecs, nb), F32),
            pltpu.VMEM((6 * vecs, p_count * nb), BF16),
            pltpu.VMEM((q_count, 6 * vecs, nb), BF16),
            pltpu.VMEM((n_rows, share, fine_cols * nb), BF16),
            pltpu.VMEM((n_rows, share, fine_cols * nb), BF16),
            dma((held, 2)),
            dma((held * n_cols,)),
            dma((held * n_cols,)),
            dma((held * n_cols,)),
            dma((held * n_cols,)),
            dma(()),
            dma(()),
            dma((n_cols,)),
            dma((n_cols,)),
            dma((n_cols,)),
            dma((n_cols,)),
            dma((n_rows,)),
            dma((n_rows,)),
        ],
        compiler_params=pltpu.CompilerParams(
            collective_id=0, has_side_effects=True, vmem_limit_bytes=52 * 1024 * 1024
        ),
        name="operator_images",
    )(
        coarse_kernel, left_rotation, right_rotation, row_pick, col_pick, mix.reshape(-1), trial_vectors
    )


def solution(mesh):
    return jax.shard_map(
        body,
        mesh=mesh,
        in_specs=(
            P(("rowk", "colk"), None, None, None),
            P("rowk", None, None, None),
            P("colk", None, None, None),
            P(),
            P("rowk", "colk", None),
            P(),
            P(None, "colk"),
        ),
        out_specs=(P(None, ("rowk", "colk")), P("rowk", "colk")),
        check_vma=False,
    )
```

time: 419 us -> 113 us (0.27)
  matrix products: 152 us -> 0 us
  Pallas kernels: 0 us -> 106 us
  local copies, waits for them, and re-layouts: 107 us -> 2.44 us
  waiting for transfers between devices: 68.5 us -> 0 us
  blocking collectives: 64.1 us -> 0 us
  between operations: 14.1 us -> 0.7 us
  other arithmetic: 7.89 us -> 3.39 us
    dot_general x18 -> x0, matrix products: 152 us -> none  [the longest x8 71.8 us: build_rows(): jnp.einsum('ipjqab,jqbc->ipjqac', picked, right_rotation, preferred_eleme...]
    pallas_call x0 -> x1, Pallas kernels: none -> 106 us  [body(): pl.pallas_call(functools.partial(operator_kernel, sizes), out_shape=(jax....]
    gather x8 -> x0, local copies, waits for them, and re-layouts: 97 us -> none  [build_rows(): local_blocks[sources[:, :, None, None], col_source[None, None, :, :]]]
    reduce_scatter x2 -> x0, waiting for transfers between devices: 57.1 us -> none  [the longest x1 37.3 us: body(): lax.psum_scatter(partial_value.astype(jnp.bfloat16), 'colk', scatter_dime...]
    all_to_all x1 -> x0, blocking collectives: 54.2 us -> none  [body(): lax.all_to_all(coarse_kernel, 'colk', split_axis=1, concat_axis=0, tiled=...]
    ppermute x2 -> x0, waiting for transfers between devices: 11.4 us -> none  [shifted(): return lax.ppermute(value, axis, pairs)]
    all_gather x1 -> x0, blocking collectives: 9.97 us -> none  [body(): row_image = lax.all_gather(forward_image, 'colk', axis=1, tiled=True)]
    concatenate x26 -> x0, other arithmetic: 7.48 us -> none  [the longest x1 5.13 us: body(): local_blocks = jnp.concatenate([taller, rim_col], axis=1)]
  transfers between devices with their start and end apart: 4 -> 0, of which waited for: 4 -> 0; matrix products, arithmetic and copies ran while one was open for 0% -> 0% of each run, Pallas kernels for 0% -> 0%
where the time goes in v1:
time: 113 us; the launch traced here: 112 us
  Pallas kernels  106 us (94%)
  other arithmetic  3.39 us (3%)
  local copies, waits for them, and re-layouts  2.44 us (2%)
    pallas_call x1, Pallas kernels, body(): pl.pallas_call(functools.partial(operator_kernel, sizes), out_shape=(jax....  106 us

profile of v1, /device:TPU:0, one launch (start us, length us, event | category | flops | bytes accessed | tf_op | source)
XLA Modules:
  0.0 112.5 jit_solution(13836911694831494917)
XLA Ops:
  0.6 0.7 fusion.5
  1.3 0.1 broadcast_add_fusion
  1.4 0.1 broadcast_add_fusion.1
  1.4 0.1 fusion.4
  1.5 0.1 fusion.2
  1.6 0.8 broadcast_compare_fusion
  2.4 1.0 select_reduce_fusion
  3.4 0.1 copy.16
  3.5 0.1 copy.13
  3.6 0.1 copy.15
  3.7 0.1 copy.14
  3.7 0.0 copy-start
  3.7 0.0 copy-start.1
  3.7 0.6 select_add_fusion
  4.4 0.1 pad.4
  4.5 0.7 reshape.90.mix_ref
  5.2 0.0 copy-done
  5.3 0.0 copy-done.1
  5.3 105.9 %operator_images.1 = (bf16[64,512]{1,0:T(8,128)(2,1)S(1)}, bf16[16,2048]{1,0:T(8,128)(2,1)S(1)}) custom-call(bf16[2,64,128,128]{3,2,1,0:T(8,128)(2,1)} %kernel_ref.1, bf16[32,2,128,128]{3,2,1,0:T(8,128)(2,1)} %left_ref.1, bf16[16,2,128,128]{3,2,1,0:T(8,128)(2,1)S(1)} %copy-done, s32[32]{0:T(128)S(1)} %get-tuple-element.5.row_pick, ...), custom_call_target="tpu_custom_call" | custom-call | tf_op jit(solution)/shard_map/operator_images/pallas_call | solution.py:347
  111.2 0.6 copy.19
  111.8 0.6 copy.20
  (1 shorter events, 0.0 us)
Async XLA Ops:
  3.7 1.5 %copy-start = (bf16[16,2,128,128]{3,2,1,0:T(8,128)(2,1)S(1)}, bf16[16,2,128,128]{3,2,1,0:T(8,128)(2,1)}, u32[]{:S(2)}) copy-start(bf16[16,2,128,128]{3,2,1,0:T(8,128)(2,1)} %right_ref.1) | copy-start | bytes 3145732
  3.7 1.5 %copy-start.1 = (bf16[64,2048]{1,0:T(8,128)(2,1)S(1)}, bf16[64,2048]{1,0:T(8,128)(2,1)}, u32[]{:S(2)}) copy-start(bf16[64,2048]{1,0:T(8,128)(2,1)} %vec_ref.1) | copy-start | bytes 786436

commit v2 on v1

v2 whole, which is shorter than its diff:
```python
import functools

import jax
import jax.numpy as jnp
from jax import lax
from jax.experimental import pallas as pl
from jax.experimental.pallas import tpu as pltpu
from jax.sharding import PartitionSpec as P

MESH = pl.DeviceIdType.MESH
F32 = jnp.float32
BF16 = jnp.bfloat16


def dot_nt(left, right):
    return lax.dot_general(left, right, (((1,), (1,)), ((), ())), preferred_element_type=F32)


def dot_nn(left, right):
    return lax.dot_general(left, right, (((1,), (0,)), ((), ())), preferred_element_type=F32)


def flip(index, bits):
    out, place = index, 1
    while place <= bits:
        if bits & place:
            out = out + place * (1 - 2 * (index // place % 2))
        place *= 2
    return out


def operator_kernel(
    sizes,
    kernel_ref, left_ref, right_ref, map_ref, index_ref, table_ref, vec_ref,
    forward_ref, adjoint_ref,
    blocks, turned, wide, partial, part_out, part_in, gathered, lifted, slots,
    back_out, back_in, mix,
    own_sem, main_send, main_recv, rim_send, rim_recv, near_send, relay_send, relay_recv,
    part_send, part_recv, row_send, row_recv, back_send, back_recv,
):
    n_rows, n_cols, held, p_count, q_count, fine_rows, fine_cols, nb, vecs = sizes
    row_id, col_id = lax.axis_index("rowk"), lax.axis_index("colk")
    coarse_cols = q_count - 1
    chunk = fine_rows // n_cols
    share = vecs // n_rows
    j_pad = fine_cols + 6
    core = col_id % 2
    sibling = flip(col_id, 1)

    far = list(range(2, n_cols))
    orders = ([1] + far, [1] + far[2:4] + far[:2] + far[4:])

    def column_peer(step):
        first, second = orders[0][step], orders[1][step]
        return (1 - core) * flip(col_id, first) + core * flip(col_id, second)

    def row_peer(offset):
        return lax.rem(row_id + offset, n_rows)

    barrier = pltpu.get_barrier_semaphore()
    for offset in range(1, n_cols):
        pl.semaphore_signal(barrier, inc=1, device_id=(row_id, flip(col_id, offset)), device_id_type=MESH)
    for offset in range(1, n_rows):
        pl.semaphore_signal(barrier, inc=1, device_id=(row_peer(offset), col_id), device_id_type=MESH)
    pl.semaphore_wait(barrier, n_cols - 1 + n_rows - 1)

    sends = []
    rims = []
    for row in range(held):
        place = col_id * held + row
        for step in range(n_cols - 1):
            peer = column_peer(step)
            rim = lax.rem(peer + 1, n_cols) * coarse_cols
            at = row * n_cols + step
            main = pltpu.make_async_remote_copy(
                src_ref=kernel_ref.at[row, pl.ds(peer * coarse_cols, coarse_cols)],
                dst_ref=blocks.at[pl.ds(0, coarse_cols), place],
                send_sem=main_send.at[at], recv_sem=main_recv.at[place],
                device_id=(row_id, peer), device_id_type=MESH,
            )
            edge = pltpu.make_async_remote_copy(
                src_ref=kernel_ref.at[row, rim], dst_ref=blocks.at[coarse_cols, place],
                send_sem=rim_send.at[at], recv_sem=rim_recv.at[place],
                device_id=(row_id, peer), device_id_type=MESH,
            )
            sends.append(main)
            main.start()
            rims.append((peer % 2 == 1, edge))
            pl.when(peer % 2 == 1)(edge.start)
    own = []
    for row in range(held):
        place = col_id * held + row
        rim = lax.rem(col_id + 1, n_cols) * coarse_cols
        own.append(pltpu.make_async_copy(
            kernel_ref.at[row, pl.ds(col_id * coarse_cols, coarse_cols)],
            blocks.at[pl.ds(0, coarse_cols), place], own_sem.at[row, 0],
        ))
        own.append(pltpu.make_async_copy(
            kernel_ref.at[row, rim], blocks.at[coarse_cols, place], own_sem.at[row, 1],
        ))
    for copy in own:
        copy.start()

    def row_base(i):
        base = map_ref[row_id * fine_rows + i] - row_id * (p_count - 1)
        return jnp.clip(base, jnp.maximum(i // 2 - 1, 0), i // 2)

    def col_base(j):
        base = map_ref[col_id * fine_cols + j] - col_id * coarse_cols
        return jnp.clip(base, jnp.maximum(j // 2 - 1, 0), j // 2)

    def mix_at(i, dp, j, slot):
        return ((i * 2 + dp) * j_pad + j) * 3 + slot

    def weigh(i, carry):
        for dp in range(2):
            for j in (0, 1, fine_cols + 2, fine_cols + 3, fine_cols + 4, fine_cols + 5):
                for slot in range(3):
                    mix[mix_at(i, dp, j, slot)] = jnp.float32(0.0)

        def one(j, inner):
            lower = col_base(j) < j // 2
            for dp in range(2):
                pair = []
                for dq in range(2):
                    entry = index_ref[(i * fine_cols + j) * 4 + 2 * dp + dq]
                    pair.append(jnp.where(entry > 0, table_ref[entry], 0.0))
                mix[mix_at(i, dp, j + 2, 0)] = jnp.where(lower, pair[0], 0.0)
                mix[mix_at(i, dp, j + 2, 1)] = jnp.where(lower, pair[1], pair[0])
                mix[mix_at(i, dp, j + 2, 2)] = jnp.where(lower, 0.0, pair[1])
            return inner

        return lax.fori_loop(0, fine_cols, one, carry)

    lax.fori_loop(0, fine_rows, weigh, 0)

    turned[...] = jnp.zeros_like(turned)
    partial[...] = jnp.zeros_like(partial)

    def turn(j, carry):
        vec = vec_ref[:, pl.ds(pl.multiple_of(j * nb, nb), nb)]
        for slot in range(3):
            side = jnp.clip(j // 2 - 1 + slot - col_base(j), 0, 1)
            turned[j + 2, slot] = dot_nt(vec, right_ref[j, side])
        return carry

    lax.fori_loop(0, fine_cols, turn, 0)

    half = vecs // 2

    def widen(step, carry):
        q, pair = step // (fine_rows // 2), step % (fine_rows // 2)
        for part in range(2):
            rows = pl.ds(part * half, half)
            tiles = [turned[2 * q + b, 2 - b // 2, rows] for b in range(6)]
            for k in range(2):
                for dp in range(2):
                    i = 2 * pair + k
                    total = mix[mix_at(i, dp, 2 * q, 2)] * tiles[0]
                    for b in range(1, 6):
                        total += mix[mix_at(i, dp, 2 * q + b, 2 - b // 2)] * tiles[b]
                    wide[i, dp, q, rows] = total.astype(BF16)
        return carry

    lax.fori_loop(0, q_count * (fine_rows // 2), widen, 0)

    def around(p, a):
        i = jnp.clip(2 * p - 2 + a, 0, fine_rows - 1)
        return i, p - row_base(i)

    def contract(p):
        bands = []
        for a in range(6):
            i, dp = around(p, a)
            side = jnp.clip(dp, 0, 1)
            bands.append(jnp.concatenate([wide[i, side, q] for q in range(q_count)], axis=1))
        matrix = jnp.concatenate([blocks[q, p] for q in range(q_count)], axis=1)
        image = dot_nt(jnp.concatenate(bands, axis=0), matrix).astype(BF16)
        for a in range(6):
            i, dp = around(p, a)
            inside = (2 * p - 2 + a == i) & (dp >= 0) & (dp <= 1)
            term = dot_nn(image[a * vecs:(a + 1) * vecs], left_ref[i, jnp.clip(dp, 0, 1)])
            partial[i] += term * jnp.where(inside, 1.0, 0.0)

    relay = pltpu.make_async_remote_copy(
        src_ref=blocks.at[:, 0], dst_ref=blocks.at[:, p_count - 1],
        send_sem=relay_send, recv_sem=relay_recv,
        device_id=(row_peer(n_rows - 1), col_id), device_id_type=MESH,
    )

    def near_copy(place):
        return pltpu.make_async_remote_copy(
            src_ref=blocks.at[0, place], dst_ref=blocks.at[coarse_cols, place],
            send_sem=near_send.at[place], recv_sem=rim_recv.at[place],
            device_id=(row_id, sibling), device_id_type=MESH,
        )

    def wait_rim(place):
        pltpu.make_async_remote_copy(
            src_ref=blocks.at[coarse_cols, place], dst_ref=blocks.at[coarse_cols, place],
            send_sem=rim_send.at[0], recv_sem=rim_recv.at[place],
            device_id=(row_id, sibling), device_id_type=MESH,
        ).wait_recv()

    def use(place):
        @pl.when(place == 0)
        def _():
            relay.start()

        contract(place)

    def take(row, offset):
        source = lax.rem(col_id // 2 + offset // 2, n_cols // 2) * 2 + lax.rem(core + offset, 2)
        place = source * held + row
        pltpu.make_async_remote_copy(
            src_ref=blocks.at[pl.ds(0, coarse_cols), place], dst_ref=blocks.at[pl.ds(0, coarse_cols), place],
            send_sem=main_send.at[0], recv_sem=main_recv.at[place],
            device_id=(row_id, source), device_id_type=MESH,
        ).wait_recv()

        @pl.when((core == 1) & (offset != 1))
        def _():
            near_copy(place).start()

        wait_rim(place)
        use(place)

    for copy in own:
        copy.wait()
    @pl.when(core == 1)
    def _():
        for row in range(held):
            near_copy(col_id * held + row).start()

    for row in range(held):
        use(col_id * held + row)

    def take_step(step, carry):
        take(step // (n_cols - 1), step % (n_cols - 1) + 1)
        return carry

    lax.fori_loop(0, held * (n_cols - 1), take_step, 0)
    relay.wait_recv()
    contract(p_count - 1)

    def part_copy(step):
        peer = column_peer(step)
        return pltpu.make_async_remote_copy(
            src_ref=part_out.at[peer], dst_ref=part_in.at[col_id],
            send_sem=part_send.at[step], recv_sem=part_recv.at[col_id],
            device_id=(row_id, peer), device_id_type=MESH,
        )

    def fill_part(target):
        for k in range(chunk):
            part_out[target, :, pl.ds(k * nb, nb)] = partial[target * chunk + k].astype(BF16)

    backwards = list(range(n_cols - 2, -1, -1))
    for step in backwards:
        fill_part(column_peer(step))
        part_copy(step).start()
    fill_part(col_id)

    total = part_out[col_id].astype(F32)
    for offset in range(1, n_cols):
        source = flip(col_id, offset)
        pltpu.make_async_remote_copy(
            src_ref=part_in.at[source], dst_ref=part_in.at[source],
            send_sem=part_send.at[0], recv_sem=part_recv.at[source],
            device_id=(row_id, source), device_id_type=MESH,
        ).wait_recv()
        total = total + part_in[source].astype(F32)
    image = total.astype(BF16)
    gathered[col_id] = image

    def row_copy(step):
        return pltpu.make_async_remote_copy(
            src_ref=gathered.at[col_id], dst_ref=gathered.at[col_id],
            send_sem=row_send.at[step], recv_sem=row_recv.at[col_id],
            device_id=(row_id, column_peer(step)), device_id_type=MESH,
        )

    for step in backwards:
        row_copy(step).start()
    forward_ref[...] = image

    def lift(source):
        for k in range(chunk):
            i = source * chunk + k
            piece = gathered[source, :, pl.ds(k * nb, nb)]
            both = dot_nt(piece, left_ref[i].reshape(2 * nb, nb)).astype(BF16)
            lifted[i, 0] = both[:, :nb]
            lifted[i, 1] = both[:, nb:]

    lift(col_id)

    def lift_next(step, carry):
        offset = step + 1
        source = lax.rem(col_id // 2 + offset // 2, n_cols // 2) * 2 + lax.rem(core + offset, 2)
        pltpu.make_async_remote_copy(
            src_ref=gathered.at[source], dst_ref=gathered.at[source],
            send_sem=row_send.at[0], recv_sem=row_recv.at[source],
            device_id=(row_id, source), device_id_type=MESH,
        ).wait_recv()
        lift(source)
        return carry

    lax.fori_loop(0, n_cols - 1, lift_next, 0)

    def spread(p, carry):
        bands = []
        for a in range(6):
            i, dp = around(p, a)
            bands.append(lifted[i, jnp.clip(dp, 0, 1)])
        matrix = jnp.concatenate([blocks[q, p] for q in range(q_count)], axis=1)
        image = dot_nn(jnp.concatenate(bands, axis=0), matrix).astype(BF16)
        for q in range(q_count):
            for a in range(6):
                slots[p, q, a] = image[a * vecs:(a + 1) * vecs, q * nb:(q + 1) * nb]
        return carry

    lax.fori_loop(0, p_count, spread, 0)

    def back_copy(piece, offset):
        peer = row_peer(offset)
        return pltpu.make_async_remote_copy(
            src_ref=back_out.at[piece, peer], dst_ref=back_in.at[piece, row_id],
            send_sem=back_send.at[piece, offset], recv_sem=back_recv.at[piece, row_id],
            device_id=(peer, col_id), device_id_type=MESH,
        )

    pieces = back_out.shape[0]
    span = fine_cols // pieces
    group = 8
    for piece in range(pieces):
        def finish(step, carry):
            j = piece * span + step
            q = col_base(j)
            slot = 1 + q - j // 2

            def add(block, totals):
                first, second = totals
                for k in range(group):
                    i = block * group + k
                    base = row_base(i)
                    for dp in range(2):
                        p = base + dp
                        a = i - 2 * p + 2
                        at = mix_at(i, dp, j + 2, slot)
                        first = first + mix[at] * slots[p, q, a].astype(F32)
                        second = second + mix[at + 1] * slots[p, q + 1, a].astype(F32)
                return first, second

            zero = jnp.zeros((vecs, nb), F32)
            first, second = lax.fori_loop(0, fine_rows // group, add, (zero, zero))
            both = jnp.concatenate([first.astype(BF16), second.astype(BF16)], axis=1)
            image = dot_nn(both, right_ref[j].reshape(2 * nb, nb))
            for target in range(n_rows):
                back_out[piece, target, :, pl.ds(pl.multiple_of(step * nb, nb), nb)] = (
                    image[target * share:(target + 1) * share].astype(BF16)
                )
            return carry

        lax.fori_loop(0, span, finish, 0)
        for offset in range(1, n_rows):
            back_copy(piece, offset).start()

    for piece in range(pieces):
        total = back_out[piece, row_id].astype(F32)
        for offset in range(1, n_rows):
            source = row_peer(offset)
            pltpu.make_async_remote_copy(
                src_ref=back_in.at[piece, source], dst_ref=back_in.at[piece, source],
                send_sem=back_send.at[piece, 0], recv_sem=back_recv.at[piece, source],
                device_id=(source, col_id), device_id_type=MESH,
            ).wait_recv()
            total = total + back_in[piece, source].astype(F32)
        adjoint_ref[:, pl.ds(piece * span * nb, span * nb)] = total.astype(BF16)

    for copy in sends:
        copy.wait_send()
    for used, copy in rims:
        pl.when(used)(copy.wait_send)

    @pl.when(core == 1)
    def _():
        def settle(step, carry):
            row, offset = step // (n_cols - 1), step % (n_cols - 1)
            offset = offset + jnp.minimum(offset, 1)
            source = lax.rem(col_id // 2 + offset // 2, n_cols // 2) * 2 + lax.rem(core + offset, 2)
            near_copy(source * held + row).wait_send()
            return carry

        lax.fori_loop(0, held * (n_cols - 1), settle, 0)

    relay.wait_send()
    for step in range(n_cols - 1):
        part_copy(step).wait_send()
        row_copy(step).wait_send()
    for piece in range(pieces):
        for offset in range(1, n_rows):
            back_copy(piece, offset).wait_send()


def body(
    coarse_kernel,
    left_rotation,
    right_rotation,
    fine_map,
    coefficient_index,
    coefficient_table,
    trial_vectors,
):
    n_rows = lax.axis_size("rowk")
    n_cols = lax.axis_size("colk")
    held, coarse_total = coarse_kernel.shape[:2]
    fine_rows = left_rotation.shape[0]
    fine_cols = right_rotation.shape[0]
    nb = left_rotation.shape[2]
    vecs = trial_vectors.shape[0]
    p_count = coarse_total // n_rows + 1
    q_count = coarse_total // n_cols + 1
    chunk = fine_rows // n_cols
    share = vecs // n_rows
    pieces = 2

    sizes = (n_rows, n_cols, held, p_count, q_count, fine_rows, fine_cols, nb, vecs)
    vmem = pl.BlockSpec(memory_space=pltpu.VMEM)
    smem = pl.BlockSpec(memory_space=pltpu.SMEM)
    dma = pltpu.SemaphoreType.DMA
    return pl.pallas_call(
        functools.partial(operator_kernel, sizes),
        out_shape=(
            jax.ShapeDtypeStruct((vecs, chunk * nb), BF16),
            jax.ShapeDtypeStruct((share, fine_cols * nb), BF16),
        ),
        in_specs=[pl.BlockSpec(memory_space=pl.ANY), vmem, vmem, smem, smem, smem, vmem],
        out_specs=(vmem, vmem),
        scratch_shapes=[
            pltpu.VMEM((q_count, p_count, nb, nb), BF16),
            pltpu.VMEM((fine_cols + 6, 3, vecs, nb), F32),
            pltpu.VMEM((fine_rows, 2, q_count, vecs, nb), BF16),
            pltpu.VMEM((fine_rows, vecs, nb), F32),
            pltpu.VMEM((n_cols, vecs, chunk * nb), BF16),
            pltpu.VMEM((n_cols, vecs, chunk * nb), BF16),
            pltpu.VMEM((n_cols, vecs, chunk * nb), BF16),
            pltpu.VMEM((fine_rows, 2, vecs, nb), BF16),
            pltpu.VMEM((p_count, q_count, 6, vecs, nb), BF16),
            pltpu.VMEM((pieces, n_rows, share, fine_cols * nb // pieces), BF16),
            pltpu.VMEM((pieces, n_rows, share, fine_cols * nb // pieces), BF16),
            pltpu.SMEM((fine_rows * 2 * (fine_cols + 6) * 3,), F32),
            dma((held, 2)),
            dma((held * n_cols,)),
            dma((p_count,)),
            dma((held * n_cols,)),
            dma((p_count,)),
            dma((p_count,)),
            dma(()),
            dma(()),
            dma((n_cols,)),
            dma((n_cols,)),
            dma((n_cols,)),
            dma((n_cols,)),
            dma((pieces, n_rows)),
            dma((pieces, n_rows)),
        ],
        compiler_params=pltpu.CompilerParams(
            collective_id=0, has_side_effects=True, vmem_limit_bytes=52 * 1024 * 1024
        ),
        name="operator_images",
    )(
        coarse_kernel, left_rotation, right_rotation, fine_map, coefficient_index.reshape(-1),
        coefficient_table, trial_vectors
    )


def solution(mesh):
    return jax.shard_map(
        body,
        mesh=mesh,
        in_specs=(
            P(("rowk", "colk"), None, None, None),
            P("rowk", None, None, None),
            P("colk", None, None, None),
            P(),
            P("rowk", "colk", None),
            P(),
            P(None, "colk"),
        ),
        out_specs=(P(None, ("rowk", "colk")), P("rowk", "colk")),
        check_vma=False,
    )
```

time: 113 us -> 106 us (0.938)
  Pallas kernels: 106 us -> 99.5 us
  local copies, waits for them, and re-layouts: 2.44 us -> 5.85 us
  other arithmetic: 3.39 us -> 0 us
    pallas_call x1, Pallas kernels: 106 us -> 99.5 us  [body(): pl.pallas_call(functools.partial(operator_kernel, sizes), out_shape=(jax....]
    unnamed x6 -> x11, local copies, waits for them, and re-layouts: 1.27 us -> 5.69 us
where the time goes in v2:
time: 106 us
  Pallas kernels  99.5 us (94%)
  local copies, waits for them, and re-layouts  5.85 us (6%)
    pallas_call x1, Pallas kernels, body(): pl.pallas_call(functools.partial(operator_kernel, sizes), out_shape=(jax....  99.5 us
    unnamed x11, local copies, waits for them, and re-layouts  5.69 us

profile of v2, /device:TPU:0, one launch (start us, length us, event | category | flops | bytes accessed | tf_op | source)
XLA Modules:
  0.0 106.0 jit_solution(3418460533134351072)
XLA Ops:
  0.6 1.0 copy.9
  1.6 0.2 reshape.7.index_ref
  1.8 0.0 copy-start
  1.8 1.2 %copy-done = bf16[16,2,128,128]{3,2,1,0:T(8,128)(2,1)S(1)} copy-done((bf16[16,2,128,128]{3,2,1,0:T(8,128)(2,1)S(1)}, bf16[16,2,128,128]{3,2,1,0:T(8,128)(2,1)}, u32[]{:S(2)}) %copy-start) | copy-done | bytes 1048600
  3.0 0.0 copy-start.1
  3.0 0.9 copy-done.1
  3.9 0.0 copy-start.2
  3.9 0.7 copy-done.2
  4.6 0.0 copy-start.3
  4.6 0.7 copy-done.3
  5.2 99.5 %operator_images.1 = (bf16[64,512]{1,0:T(8,128)(2,1)S(1)}, bf16[16,2048]{1,0:T(8,128)(2,1)S(1)}) custom-call(bf16[2,64,128,128]{3,2,1,0:T(8,128)(2,1)} %kernel_ref.1, bf16[32,2,128,128]{3,2,1,0:T(8,128)(2,1)} %left_ref.1, bf16[16,2,128,128]{3,2,1,0:T(8,128)(2,1)S(1)} %copy-done, s32[128]{0:T(128)S(1)} %copy-done.2, s32[2048]{0:T(1024)S(1)} %reshape.7.index_ref, ...), custom_call_target="tpu_custom_call" | custom-call | tf_op jit(solution)/shard_map/operator_images/pallas_call | solution.py:431
  104.7 0.6 copy.12
  105.3 0.6 copy.13
Async XLA Ops:
  1.8 1.2 %copy-start = (bf16[16,2,128,128]{3,2,1,0:T(8,128)(2,1)S(1)}, bf16[16,2,128,128]{3,2,1,0:T(8,128)(2,1)}, u32[]{:S(2)}) copy-start(bf16[16,2,128,128]{3,2,1,0:T(8,128)(2,1)} %right_ref.1) | copy-start | bytes 3145732
  3.0 0.9 copy-start.1
  3.9 0.7 copy-start.2
  4.6 0.7 copy-start.3

commit v3 on v2

--- a/solution.py
+++ b/solution.py
@@ -31,11 +31,11 @@
 
 def operator_kernel(
     sizes,
-    kernel_ref, left_ref, right_ref, map_ref, index_ref, table_ref, vec_ref,
+    kernel_ref, left_far, right_far, map_ref, index_ref, table_ref, vec_far,
     forward_ref, adjoint_ref,
     blocks, turned, wide, partial, part_out, part_in, gathered, lifted, slots,
-    back_out, back_in, mix,
-    own_sem, main_send, main_recv, rim_send, rim_recv, near_send, relay_send, relay_recv,
+    back_out, back_in, left_ref, right_ref, vec_ref, mix_rows, mix, spot,
+    own_sem, load_sem, mix_sem, main_send, main_recv, rim_send, rim_recv, near_send, relay_send, relay_recv,
     part_send, part_recv, row_send, row_recv, back_send, back_recv,
 ):
     n_rows, n_cols, held, p_count, q_count, fine_rows, fine_cols, nb, vecs = sizes
@@ -100,6 +100,12 @@
         ))
     for copy in own:
         copy.start()
+    loads = [
+        pltpu.make_async_copy(far_ref, near_ref, load_sem.at[at])
+        for at, (far_ref, near_ref) in enumerate(((vec_far, vec_ref), (right_far, right_ref), (left_far, left_ref)))
+    ]
+    for copy in loads:
+        copy.start()
 
     def row_base(i):
         base = map_ref[row_id * fine_rows + i] - row_id * (p_count - 1)
@@ -109,30 +115,30 @@
         base = map_ref[col_id * fine_cols + j] - col_id * coarse_cols
         return jnp.clip(base, jnp.maximum(j // 2 - 1, 0), j // 2)
 
-    def mix_at(i, dp, j, slot):
-        return ((i * 2 + dp) * j_pad + j) * 3 + slot
-
-    def weigh(i, carry):
+    mix_rows[...] = jnp.zeros_like(mix_rows)
+
+    def weigh(j, carry):
+        entry = index_ref[j]
+        weight = jnp.zeros(entry.shape, F32)
+        for k in range(1, table_ref.shape[0]):
+            weight = jnp.where(entry == k, table_ref[k], weight)
+        lower = jnp.where(col_base(j) < j // 2, 1.0, 0.0)
         for dp in range(2):
-            for j in (0, 1, fine_cols + 2, fine_cols + 3, fine_cols + 4, fine_cols + 5):
-                for slot in range(3):
-                    mix[mix_at(i, dp, j, slot)] = jnp.float32(0.0)
-
-        def one(j, inner):
-            lower = col_base(j) < j // 2
-            for dp in range(2):
-                pair = []
-                for dq in range(2):
-                    entry = index_ref[(i * fine_cols + j) * 4 + 2 * dp + dq]
-                    pair.append(jnp.where(entry > 0, table_ref[entry], 0.0))
-                mix[mix_at(i, dp, j + 2, 0)] = jnp.where(lower, pair[0], 0.0)
-                mix[mix_at(i, dp, j + 2, 1)] = jnp.where(lower, pair[1], pair[0])
-                mix[mix_at(i, dp, j + 2, 2)] = jnp.where(lower, 0.0, pair[1])
-            return inner
-
-        return lax.fori_loop(0, fine_cols, one, carry)
-
-    lax.fori_loop(0, fine_rows, weigh, 0)
+            near, next_one = weight[2 * dp:2 * dp + 1], weight[2 * dp + 1:2 * dp + 2]
+            values = (lower * near, lower * next_one + (1.0 - lower) * near, (1.0 - lower) * next_one)
+            for slot in range(3):
+                mix_rows[pl.ds((j + 2) * 8 + dp * 3 + slot, 1), pl.ds(0, fine_rows)] = values[slot]
+        return carry
+
+    lax.fori_loop(0, fine_cols, weigh, 0)
+    mix_copy = pltpu.make_async_copy(mix_rows, mix, mix_sem)
+    mix_copy.start()
+
+    def locate(i, carry):
+        spot[i] = 4 * row_base(i) + i + 8
+        return carry
+
+    lax.fori_loop(0, fine_rows, locate, 0)
 
     turned[...] = jnp.zeros_like(turned)
     partial[...] = jnp.zeros_like(partial)
@@ -144,25 +150,37 @@
             turned[j + 2, slot] = dot_nt(vec, right_ref[j, side])
         return carry
 
+    for copy in loads:
+        copy.wait()
     lax.fori_loop(0, fine_cols, turn, 0)
+    mix_copy.wait()
 
     half = vecs // 2
 
-    def widen(step, carry):
-        q, pair = step // (fine_rows // 2), step % (fine_rows // 2)
+    def widen(q, pair, count):
         for part in range(2):
             rows = pl.ds(part * half, half)
-            tiles = [turned[2 * q + b, 2 - b // 2, rows] for b in range(6)]
+            tiles = [turned[2 * q + b, 2 - b // 2, rows] for b in range(count)]
             for k in range(2):
                 for dp in range(2):
                     i = 2 * pair + k
-                    total = mix[mix_at(i, dp, 2 * q, 2)] * tiles[0]
-                    for b in range(1, 6):
-                        total += mix[mix_at(i, dp, 2 * q + b, 2 - b // 2)] * tiles[b]
+                    total = mix[2 * q * 8 + dp * 3 + 2, i] * tiles[0]
+                    for b in range(1, count):
+                        total += mix[(2 * q + b) * 8 + dp * 3 + 2 - b // 2, i] * tiles[b]
                     wide[i, dp, q, rows] = total.astype(BF16)
-        return carry
-
-    lax.fori_loop(0, q_count * (fine_rows // 2), widen, 0)
+
+    pairs = fine_rows // 2
+
+    def widen_step(step, carry):
+        widen(step // pairs, step % pairs, 6)
+        return carry
+
+    def widen_last(pair, carry):
+        widen(coarse_cols, pair, 2)
+        return carry
+
+    lax.fori_loop(0, coarse_cols * pairs, widen_step, 0)
+    lax.fori_loop(0, pairs, widen_last, 0)
 
     def around(p, a):
         i = jnp.clip(2 * p - 2 + a, 0, fine_rows - 1)
@@ -285,12 +303,28 @@
     forward_ref[...] = image
 
     def lift(source):
-        for k in range(chunk):
-            i = source * chunk + k
-            piece = gathered[source, :, pl.ds(k * nb, nb)]
-            both = dot_nt(piece, left_ref[i].reshape(2 * nb, nb)).astype(BF16)
-            lifted[i, 0] = both[:, :nb]
-            lifted[i, 1] = both[:, nb:]
+        for k in range(0, chunk, 2):
+            bands = []
+            for i in (source * chunk + k, source * chunk + k + 1):
+                piece = gathered[source, :, pl.ds((k + len(bands)) * nb, nb)]
+                bands.append(dot_nt(piece, left_ref[i].reshape(2 * nb, nb)).astype(BF16))
+            for member in range(2):
+                lifted[source * chunk + k + member, 0] = bands[member][:, :nb]
+                lifted[source * chunk + k + member, 1] = bands[member][:, nb:]
+            point = source * chunk + k
+            above = point // 2
+            for slot in range(3):
+                p = above - 1 + slot
+                picked = [
+                    lifted[point + member, jnp.clip(p - row_base(point + member), 0, 1)] for member in range(2)
+                ]
+                place = jnp.maximum(p, 0)
+                matrix = jnp.concatenate([blocks[q, place] for q in range(q_count)], axis=1)
+                image = dot_nn(jnp.concatenate(picked, axis=0), matrix).astype(BF16)
+                at = p * 6 + 6 + (2 - slot) * 2
+                for member in range(2):
+                    for q in range(q_count):
+                        slots[at + member, q] = image[member * vecs:(member + 1) * vecs, q * nb:(q + 1) * nb]
 
     lift(col_id)
 
@@ -307,20 +341,6 @@
 
     lax.fori_loop(0, n_cols - 1, lift_next, 0)
 
-    def spread(p, carry):
-        bands = []
-        for a in range(6):
-            i, dp = around(p, a)
-            bands.append(lifted[i, jnp.clip(dp, 0, 1)])
-        matrix = jnp.concatenate([blocks[q, p] for q in range(q_count)], axis=1)
-        image = dot_nn(jnp.concatenate(bands, axis=0), matrix).astype(BF16)
-        for q in range(q_count):
-            for a in range(6):
-                slots[p, q, a] = image[a * vecs:(a + 1) * vecs, q * nb:(q + 1) * nb]
-        return carry
-
-    lax.fori_loop(0, p_count, spread, 0)
-
     def back_copy(piece, offset):
         peer = row_peer(offset)
         return pltpu.make_async_remote_copy(
@@ -342,13 +362,11 @@
                 first, second = totals
                 for k in range(group):
                     i = block * group + k
-                    base = row_base(i)
+                    at = spot[i]
                     for dp in range(2):
-                        p = base + dp
-                        a = i - 2 * p + 2
-                        at = mix_at(i, dp, j + 2, slot)
-                        first = first + mix[at] * slots[p, q, a].astype(F32)
-                        second = second + mix[at + 1] * slots[p, q + 1, a].astype(F32)
+                        row = (j + 2) * 8 + slot + dp * 3
+                        first = first + mix[row, i] * slots[at + 4 * dp, q].astype(F32)
+                        second = second + mix[row + 1, i] * slots[at + 4 * dp, q + 1].astype(F32)
                 return first, second
 
             zero = jnp.zeros((vecs, nb), F32)
@@ -425,6 +443,7 @@
     pieces = 2
 
     sizes = (n_rows, n_cols, held, p_count, q_count, fine_rows, fine_cols, nb, vecs)
+    anywhere = pl.BlockSpec(memory_space=pltpu.HBM)
     vmem = pl.BlockSpec(memory_space=pltpu.VMEM)
     smem = pl.BlockSpec(memory_space=pltpu.SMEM)
     dma = pltpu.SemaphoreType.DMA
@@ -434,7 +453,7 @@
             jax.ShapeDtypeStruct((vecs, chunk * nb), BF16),
             jax.ShapeDtypeStruct((share, fine_cols * nb), BF16),
         ),
-        in_specs=[pl.BlockSpec(memory_space=pl.ANY), vmem, vmem, smem, smem, smem, vmem],
+        in_specs=[anywhere, anywhere, anywhere, smem, vmem, smem, anywhere],
         out_specs=(vmem, vmem),
         scratch_shapes=[
             pltpu.VMEM((q_count, p_count, nb, nb), BF16),
@@ -445,11 +464,18 @@
             pltpu.VMEM((n_cols, vecs, chunk * nb), BF16),
             pltpu.VMEM((n_cols, vecs, chunk * nb), BF16),
             pltpu.VMEM((fine_rows, 2, vecs, nb), BF16),
-            pltpu.VMEM((p_count, q_count, 6, vecs, nb), BF16),
+            pltpu.VMEM((p_count * 6 + 6, q_count, vecs, nb), BF16),
             pltpu.VMEM((pieces, n_rows, share, fine_cols * nb // pieces), BF16),
             pltpu.VMEM((pieces, n_rows, share, fine_cols * nb // pieces), BF16),
-            pltpu.SMEM((fine_rows * 2 * (fine_cols + 6) * 3,), F32),
+            pltpu.VMEM(left_rotation.shape, BF16),
+            pltpu.VMEM(right_rotation.shape, BF16),
+            pltpu.VMEM(trial_vectors.shape, BF16),
+            pltpu.VMEM(((fine_cols + 6) * 8, 128), F32),
+            pltpu.SMEM(((fine_cols + 6) * 8, 128), F32),
+            pltpu.SMEM((fine_rows,), jnp.int32),
             dma((held, 2)),
+            dma((3,)),
+            dma(()),
             dma((held * n_cols,)),
             dma((p_count,)),
             dma((held * n_cols,)),
@@ -469,7 +495,7 @@
         ),
         name="operator_images",
     )(
-        coarse_kernel, left_rotation, right_rotation, fine_map, coefficient_index.reshape(-1),
+        coarse_kernel, left_rotation, right_rotation, fine_map, coefficient_index.transpose(1, 2, 0),
         coefficient_table, trial_vectors
     )
 

time: 106 us -> 99.9 us (0.942)
  Pallas kernels: 99.5 us -> 93.5 us
    pallas_call x1, Pallas kernels: 99.5 us -> 93.5 us  [body(): pl.pallas_call(functools.partial(operator_kernel, sizes), out_shape=(jax....]
    unnamed x11 -> x12, local copies, waits for them, and re-layouts: 5.69 us -> 5.5 us
where the time goes in v3:
time: 99.9 us; the launch traced here: 99.6 us
  Pallas kernels  93.5 us (94%)
  local copies, waits for them, and re-layouts  5.5 us (6%)
    pallas_call x1, Pallas kernels, body(): pl.pallas_call(functools.partial(operator_kernel, sizes), out_shape=(jax....  93.5 us
    unnamed x12, local copies, waits for them, and re-layouts  5.5 us

profile of v3, /device:TPU:0, one launch (start us, length us, event | category | flops | bytes accessed | tf_op | source)
XLA Modules:
  0.0 99.6 jit_solution(941805914777199713)
XLA Ops:
  0.6 0.0 copy-start
  0.6 1.2 %copy-done = bf16[16,2,128,128]{3,2,1,0:T(8,128)(2,1)S(1)} copy-done((bf16[16,2,128,128]{3,2,1,0:T(8,128)(2,1)S(1)}, bf16[16,2,128,128]{3,2,1,0:T(8,128)(2,1)}, u32[]{:S(2)}) %copy-start) | copy-done | bytes 1048600
  1.9 0.0 copy-start.1
  1.9 0.9 copy-done.1
  2.8 0.0 copy-start.2
  2.8 0.8 copy-done.2
  3.6 0.0 copy-start.3
  3.6 0.7 copy-done.3
  4.2 0.0 copy-start.4
  4.2 0.7 copy-done.4
  4.9 93.5 %operator_images.1 = (bf16[64,512]{1,0:T(8,128)(2,1)S(1)}, bf16[16,2048]{1,0:T(8,128)(2,1)S(1)}) custom-call(bf16[2,64,128,128]{3,2,1,0:T(8,128)(2,1)} %kernel_ref.1, bf16[32,2,128,128]{3,2,1,0:T(8,128)(2,1)} %left_far.1, bf16[16,2,128,128]{3,2,1,0:T(8,128)(2,1)S(1)} %copy-done, s32[128]{0:T(128)S(1)} %copy-done.3, s32[16,4,32]{2,1,0:T(4,128)S(1)} %bitcast.1, ...), custom_call_target="tpu_custom_call" | custom-call | tf_op jit(solution)/shard_map/operator_images/pallas_call | solution.py:450
  98.3 0.6 copy.11
  99.0 0.6 copy.12
Async XLA Ops:
  0.6 1.2 %copy-start = (bf16[16,2,128,128]{3,2,1,0:T(8,128)(2,1)S(1)}, bf16[16,2,128,128]{3,2,1,0:T(8,128)(2,1)}, u32[]{:S(2)}) copy-start(bf16[16,2,128,128]{3,2,1,0:T(8,128)(2,1)} %right_far.1) | copy-start | bytes 3145732
  1.9 0.9 copy-start.1
  2.8 0.8 copy-start.2
  3.6 0.7 copy-start.3
  4.2 0.7 copy-start.4

commit v4 on v3

--- a/solution.py
+++ b/solution.py
@@ -64,29 +64,69 @@
         pl.semaphore_signal(barrier, inc=1, device_id=(row_peer(offset), col_id), device_id_type=MESH)
     pl.semaphore_wait(barrier, n_cols - 1 + n_rows - 1)
 
-    sends = []
-    rims = []
+    far_count = n_cols - 2
+    window = 4
+    copies = held * far_count
+
+    def far_peer(at, turn_of):
+        step = at % far_count
+        chip, other = step // 2, step % 2
+        first = jnp.where(chip < 2, 1 - chip, chip) * turn_of + chip * (1 - turn_of) + 1
+        mine, found, place = col_id // 2, 0, 1
+        while place < n_cols // 2:
+            left, right = first // place % 2, mine // place % 2
+            found = found + place * (left + right - 2 * left * right)
+            place *= 2
+        return found * 2 + core + other * (1 - 2 * core)
+
+    def coarse_copy(row, peer, at):
+        return pltpu.make_async_remote_copy(
+            src_ref=kernel_ref.at[row, pl.ds(peer * coarse_cols, coarse_cols)],
+            dst_ref=blocks.at[pl.ds(0, coarse_cols), col_id * held + row],
+            send_sem=main_send.at[at], recv_sem=main_recv.at[col_id * held + row],
+            device_id=(row_id, peer), device_id_type=MESH,
+        )
+
+    def edge_copy(row, peer, at):
+        rim = lax.rem(peer + 1, n_cols) * coarse_cols
+        return pltpu.make_async_remote_copy(
+            src_ref=kernel_ref.at[row, rim], dst_ref=blocks.at[coarse_cols, col_id * held + row],
+            send_sem=rim_send.at[at], recv_sem=rim_recv.at[col_id * held + row],
+            device_id=(row_id, peer), device_id_type=MESH,
+        )
+
+    def start_far(at):
+        peer = far_peer(at, core)
+        row = at // far_count
+        coarse_copy(row, peer, at).start()
+
+        @pl.when(peer % 2 == 1)
+        def _():
+            edge_copy(row, peer, at).start()
+
+    def wait_far(at):
+        peer = far_peer(at, core)
+        row = at // far_count
+        coarse_copy(row, peer, at).wait_send()
+
+        @pl.when(peer % 2 == 1)
+        def _():
+            edge_copy(row, peer, at).wait_send()
+
+    def advance(at):
+        wait_far(at)
+        start_far(at + window)
+
+    for at in range(window):
+        start_far(at)
     for row in range(held):
-        place = col_id * held + row
-        for step in range(n_cols - 1):
-            peer = column_peer(step)
-            rim = lax.rem(peer + 1, n_cols) * coarse_cols
-            at = row * n_cols + step
-            main = pltpu.make_async_remote_copy(
-                src_ref=kernel_ref.at[row, pl.ds(peer * coarse_cols, coarse_cols)],
-                dst_ref=blocks.at[pl.ds(0, coarse_cols), place],
-                send_sem=main_send.at[at], recv_sem=main_recv.at[place],
-                device_id=(row_id, peer), device_id_type=MESH,
-            )
-            edge = pltpu.make_async_remote_copy(
-                src_ref=kernel_ref.at[row, rim], dst_ref=blocks.at[coarse_cols, place],
-                send_sem=rim_send.at[at], recv_sem=rim_recv.at[place],
-                device_id=(row_id, peer), device_id_type=MESH,
-            )
-            sends.append(main)
-            main.start()
-            rims.append((peer % 2 == 1, edge))
-            pl.when(peer % 2 == 1)(edge.start)
+        coarse_copy(row, sibling, copies + row).start()
+
+    @pl.when(core == 0)
+    def _():
+        for row in range(held):
+            edge_copy(row, sibling, copies + row).start()
+
     own = []
     for row in range(held):
         place = col_id * held + row
@@ -179,7 +219,11 @@
         widen(coarse_cols, pair, 2)
         return carry
 
-    lax.fori_loop(0, coarse_cols * pairs, widen_step, 0)
+    early = 3
+    bounds = [0] + [(coarse_cols - early + k + 1) * pairs for k in range(early)]
+    for k in range(early):
+        lax.fori_loop(bounds[k], bounds[k + 1], widen_step, 0)
+        advance(k)
     lax.fori_loop(0, pairs, widen_last, 0)
 
     def around(p, a):
@@ -227,8 +271,7 @@
 
         contract(place)
 
-    def take(row, offset):
-        source = lax.rem(col_id // 2 + offset // 2, n_cols // 2) * 2 + lax.rem(core + offset, 2)
+    def take(row, source):
         place = source * held + row
         pltpu.make_async_remote_copy(
             src_ref=blocks.at[pl.ds(0, coarse_cols), place], dst_ref=blocks.at[pl.ds(0, coarse_cols), place],
@@ -236,7 +279,7 @@
             device_id=(row_id, source), device_id_type=MESH,
         ).wait_recv()
 
-        @pl.when((core == 1) & (offset != 1))
+        @pl.when((core == 1) & (source != sibling))
         def _():
             near_copy(place).start()
 
@@ -253,11 +296,18 @@
     for row in range(held):
         use(col_id * held + row)
 
-    def take_step(step, carry):
-        take(step // (n_cols - 1), step % (n_cols - 1) + 1)
-        return carry
-
-    lax.fori_loop(0, held * (n_cols - 1), take_step, 0)
+    for row in range(held):
+        take(row, sibling)
+
+    def take_step(at, carry):
+        @pl.when(at + early < copies - window)
+        def _():
+            advance(at + early)
+
+        take(at // far_count, far_peer(at, core))
+        return carry
+
+    lax.fori_loop(0, copies, take_step, 0)
     relay.wait_recv()
     contract(p_count - 1)
 
@@ -395,21 +445,30 @@
             total = total + back_in[piece, source].astype(F32)
         adjoint_ref[:, pl.ds(piece * span * nb, span * nb)] = total.astype(BF16)
 
-    for copy in sends:
-        copy.wait_send()
-    for used, copy in rims:
-        pl.when(used)(copy.wait_send)
+    for row in range(held):
+        coarse_copy(row, sibling, copies + row).wait_send()
+
+    @pl.when(core == 0)
+    def _():
+        for row in range(held):
+            edge_copy(row, sibling, copies + row).wait_send()
+
+    def settle(at, carry):
+        wait_far(at)
+        return carry
+
+    lax.fori_loop(copies - window, copies, settle, 0)
 
     @pl.when(core == 1)
     def _():
-        def settle(step, carry):
-            row, offset = step // (n_cols - 1), step % (n_cols - 1)
-            offset = offset + jnp.minimum(offset, 1)
-            source = lax.rem(col_id // 2 + offset // 2, n_cols // 2) * 2 + lax.rem(core + offset, 2)
-            near_copy(source * held + row).wait_send()
+        for row in range(held):
+            near_copy(col_id * held + row).wait_send()
+
+        def settle_near(at, carry):
+            near_copy(far_peer(at, core) * held + at // far_count).wait_send()
             return carry
 
-        lax.fori_loop(0, held * (n_cols - 1), settle, 0)
+        lax.fori_loop(0, copies, settle_near, 0)
 
     relay.wait_send()
     for step in range(n_cols - 1):
@@ -440,7 +499,7 @@
     q_count = coarse_total // n_cols + 1
     chunk = fine_rows // n_cols
     share = vecs // n_rows
-    pieces = 2
+    pieces = 4
 
     sizes = (n_rows, n_cols, held, p_count, q_count, fine_rows, fine_cols, nb, vecs)
     anywhere = pl.BlockSpec(memory_space=pltpu.HBM)

time: 99.9 us -> 101 us (1.011)
  no operation moved by 1% of the time
where the time goes in v4:
time: 101 us; the launch traced here: 100 us
  Pallas kernels  94.2 us (93%)
  local copies, waits for them, and re-layouts  5.5 us (5%)
    pallas_call x1, Pallas kernels, body(): pl.pallas_call(functools.partial(operator_kernel, sizes), out_shape=(jax....  94.2 us
    unnamed x12, local copies, waits for them, and re-layouts  5.5 us

profile of v4, /device:TPU:0, one launch (start us, length us, event | category | flops | bytes accessed | tf_op | source)
XLA Modules:
  0.0 100.3 jit_solution(17060716622992175439)
XLA Ops:
  0.6 0.0 copy-start
  0.6 1.2 %copy-done = bf16[16,2,128,128]{3,2,1,0:T(8,128)(2,1)S(1)} copy-done((bf16[16,2,128,128]{3,2,1,0:T(8,128)(2,1)S(1)}, bf16[16,2,128,128]{3,2,1,0:T(8,128)(2,1)}, u32[]{:S(2)}) %copy-start) | copy-done | bytes 1048600
  1.9 0.0 copy-start.1
  1.9 0.9 copy-done.1
  2.8 0.0 copy-start.2
  2.8 0.8 copy-done.2
  3.6 0.0 copy-start.3
  3.6 0.7 copy-done.3
  4.2 0.0 copy-start.4
  4.2 0.7 copy-done.4
  4.9 94.2 %operator_images.1 = (bf16[64,512]{1,0:T(8,128)(2,1)S(1)}, bf16[16,2048]{1,0:T(8,128)(2,1)S(1)}) custom-call(bf16[2,64,128,128]{3,2,1,0:T(8,128)(2,1)} %kernel_ref.1, bf16[32,2,128,128]{3,2,1,0:T(8,128)(2,1)} %left_far.1, bf16[16,2,128,128]{3,2,1,0:T(8,128)(2,1)S(1)} %copy-done, s32[128]{0:T(128)S(1)} %copy-done.3, s32[16,4,32]{2,1,0:T(4,128)S(1)} %bitcast.1, ...), custom_call_target="tpu_custom_call" | custom-call | tf_op jit(solution)/shard_map/operator_images/pallas_call | solution.py:509
  99.1 0.6 copy.11
  99.7 0.6 copy.12
Async XLA Ops:
  0.6 1.2 %copy-start = (bf16[16,2,128,128]{3,2,1,0:T(8,128)(2,1)S(1)}, bf16[16,2,128,128]{3,2,1,0:T(8,128)(2,1)}, u32[]{:S(2)}) copy-start(bf16[16,2,128,128]{3,2,1,0:T(8,128)(2,1)} %right_far.1) | copy-start | bytes 3145732
  1.9 0.9 copy-start.1
  2.8 0.8 copy-start.2
  3.6 0.7 copy-start.3
  4.2 0.7 copy-start.4

commit v5 on v3

--- a/solution.py
+++ b/solution.py
@@ -141,13 +141,13 @@
     lax.fori_loop(0, fine_rows, locate, 0)
 
     turned[...] = jnp.zeros_like(turned)
-    partial[...] = jnp.zeros_like(partial)
 
     def turn(j, carry):
         vec = vec_ref[:, pl.ds(pl.multiple_of(j * nb, nb), nb)]
-        for slot in range(3):
-            side = jnp.clip(j // 2 - 1 + slot - col_base(j), 0, 1)
-            turned[j + 2, slot] = dot_nt(vec, right_ref[j, side])
+        both = dot_nt(vec, right_ref[j].reshape(2 * nb, nb))
+        turned[j + 2, 0] = both[:, :nb]
+        turned[j + 2, 1] = jnp.where(col_base(j) < j // 2, both[:, nb:], both[:, :nb])
+        turned[j + 2, 2] = both[:, nb:]
         return carry
 
     for copy in loads:
@@ -195,10 +195,7 @@
         matrix = jnp.concatenate([blocks[q, p] for q in range(q_count)], axis=1)
         image = dot_nt(jnp.concatenate(bands, axis=0), matrix).astype(BF16)
         for a in range(6):
-            i, dp = around(p, a)
-            inside = (2 * p - 2 + a == i) & (dp >= 0) & (dp <= 1)
-            term = dot_nn(image[a * vecs:(a + 1) * vecs], left_ref[i, jnp.clip(dp, 0, 1)])
-            partial[i] += term * jnp.where(inside, 1.0, 0.0)
+            partial[p * 6 + a] = image[a * vecs:(a + 1) * vecs]
 
     relay = pltpu.make_async_remote_copy(
         src_ref=blocks.at[:, 0], dst_ref=blocks.at[:, p_count - 1],
@@ -271,7 +268,10 @@
 
     def fill_part(target):
         for k in range(chunk):
-            part_out[target, :, pl.ds(k * nb, nb)] = partial[target * chunk + k].astype(BF16)
+            i = target * chunk + k
+            at = spot[i] - 6
+            pair = jnp.concatenate([partial[at], partial[at + 4]], axis=1)
+            part_out[target, :, pl.ds(k * nb, nb)] = dot_nn(pair, left_ref[i].reshape(2 * nb, nb)).astype(BF16)
 
     backwards = list(range(n_cols - 2, -1, -1))
     for step in backwards:
@@ -440,7 +440,7 @@
     q_count = coarse_total // n_cols + 1
     chunk = fine_rows // n_cols
     share = vecs // n_rows
-    pieces = 2
+    pieces = 4
 
     sizes = (n_rows, n_cols, held, p_count, q_count, fine_rows, fine_cols, nb, vecs)
     anywhere = pl.BlockSpec(memory_space=pltpu.HBM)
@@ -459,7 +459,7 @@
             pltpu.VMEM((q_count, p_count, nb, nb), BF16),
             pltpu.VMEM((fine_cols + 6, 3, vecs, nb), F32),
             pltpu.VMEM((fine_rows, 2, q_count, vecs, nb), BF16),
-            pltpu.VMEM((fine_rows, vecs, nb), F32),
+            pltpu.VMEM((p_count * 6, vecs, nb), BF16),
             pltpu.VMEM((n_cols, vecs, chunk * nb), BF16),
             pltpu.VMEM((n_cols, vecs, chunk * nb), BF16),
             pltpu.VMEM((n_cols, vecs, chunk * nb), BF16),

time: 99.9 us -> 99.6 us (level)
  no operation moved by 1% of the time
where the time goes in v5:
time: 99.6 us; the launch traced here: 99.3 us
  Pallas kernels  93.1 us (93%)
  local copies, waits for them, and re-layouts  5.5 us (6%)
    pallas_call x1, Pallas kernels, body(): pl.pallas_call(functools.partial(operator_kernel, sizes), out_shape=(jax....  93.1 us
    unnamed x12, local copies, waits for them, and re-layouts  5.5 us

profile of v5, /device:TPU:0, one launch (start us, length us, event | category | flops | bytes accessed | tf_op | source)
XLA Modules:
  0.0 99.3 jit_solution(6877769310908370382)
XLA Ops:
  0.6 0.0 copy-start
  0.6 1.2 %copy-done = bf16[16,2,128,128]{3,2,1,0:T(8,128)(2,1)S(1)} copy-done((bf16[16,2,128,128]{3,2,1,0:T(8,128)(2,1)S(1)}, bf16[16,2,128,128]{3,2,1,0:T(8,128)(2,1)}, u32[]{:S(2)}) %copy-start) | copy-done | bytes 1048600
  1.9 0.0 copy-start.1
  1.9 0.9 copy-done.1
  2.8 0.0 copy-start.2
  2.8 0.8 copy-done.2
  3.6 0.0 copy-start.3
  3.6 0.7 copy-done.3
  4.2 0.0 copy-start.4
  4.2 0.7 copy-done.4
  4.9 93.1 %operator_images.1 = (bf16[64,512]{1,0:T(8,128)(2,1)S(1)}, bf16[16,2048]{1,0:T(8,128)(2,1)S(1)}) custom-call(bf16[2,64,128,128]{3,2,1,0:T(8,128)(2,1)} %kernel_ref.1, bf16[32,2,128,128]{3,2,1,0:T(8,128)(2,1)} %left_far.1, bf16[16,2,128,128]{3,2,1,0:T(8,128)(2,1)S(1)} %copy-done, s32[128]{0:T(128)S(1)} %copy-done.3, s32[16,4,32]{2,1,0:T(4,128)S(1)} %bitcast.1, ...), custom_call_target="tpu_custom_call" | custom-call | tf_op jit(solution)/shard_map/operator_images/pallas_call | solution.py:450
  98.0 0.6 copy.11
  98.6 0.6 copy.12
Async XLA Ops:
  0.6 1.2 %copy-start = (bf16[16,2,128,128]{3,2,1,0:T(8,128)(2,1)S(1)}, bf16[16,2,128,128]{3,2,1,0:T(8,128)(2,1)}, u32[]{:S(2)}) copy-start(bf16[16,2,128,128]{3,2,1,0:T(8,128)(2,1)} %right_far.1) | copy-start | bytes 3145732
  1.9 0.9 copy-start.1
  2.8 0.8 copy-start.2
  3.6 0.7 copy-start.3
  4.2 0.7 copy-start.4
